TPU v7x, 256 devices: a whole 4x4x8 slice. The times are simulated.
256 devices in a mesh: lat: 16 (over z, y_hi), lon: 16 (over x, y_lo, core).
Axes of the slice: x: 4, y: 4 (y_hi: 2, y_lo: 2; y = y_hi * 2 + y_lo), z: 8, core: 2. Of those that a mesh axis runs over, the one named last changes fastest.
Arguments:
- fields: bfloat16 [128, 1440, 256], P('lat', 'lon'), may hold values from -6 to 6
- lat_mask: int32 [128], P('lat'), may hold values from 0 to 1, as said below
- conv_first: bfloat16 [2, 3, 3, 256, 256], replicated, may hold values from -0.125 to 0.125
- conv_second: bfloat16 [2, 3, 3, 256, 256], replicated, may hold values from -0.125 to 0.125
- norm_gain: float32 [2, 256], replicated, may hold values from 0.1 to 1.9
- qkv_weight: bfloat16 [2, 256, 768], replicated, may hold values from -0.375 to 0.375
- out_weight: bfloat16 [2, 256, 256], replicated, may hold values from -1.5 to 1.5
Outputs:
- result: bfloat16 [128, 1440, 256], P('lat', 'lon')
Inputs may be any that keep to these rules, and one draw needn't show every extreme that they name: lat_mask is 1 on the first latitude rows and 0 on the rest; between 1 and 12 rows are 0.
All inputs are finite; a program needn't handle non-finite values.
Results may differ from a plain program's by a relative error of at most 0.013.
Values may be sent and summed in bfloat16 or wider, within the bound.
A program may use at most 128 MiB of HBM per device.

v0:
```python
import jax
import jax.numpy as jnp
from jax import lax
from jax.sharding import PartitionSpec as P

HEADS = 4
BLOCKS = 2


def padded_2(cells, sides, width, closed):
    for axis, dim in sides:
        count = lax.axis_size(axis)
        ends = count if closed else count - 1
        head = lax.slice_in_dim(cells, 0, width, axis=dim)
        tail = lax.slice_in_dim(cells, cells.shape[dim] - width, cells.shape[dim], axis=dim)
        cells = jnp.concatenate(
            [
                lax.ppermute(tail, axis, [(i, (i + 1) % count) for i in range(ends)]),
                cells,
                lax.ppermute(head, axis, [((i + 1) % count, i) for i in range(ends)]),
            ],
            axis=dim,
        )
    return cells


def rims_single(values):
    banded = padded_2(values, (("lat", 0),), 1, False)
    return padded_2(banded, (("lon", 1),), 1, True)


def rims_double(values):
    banded = padded_2(values, (("lat", 0),), 2, False)
    return padded_2(banded, (("lon", 1),), 2, True)


def convolve(padded, kernel, spread, rows, cols):
    total = jnp.zeros((rows, cols, kernel.shape[3]), jnp.float32)
    for i in range(3):
        for j in range(3):
            window = padded[i * spread : i * spread + rows, j * spread : j * spread + cols]
            total = total + jnp.dot(window, kernel[i, j], preferred_element_type=jnp.float32)
    return total


def attend_keys(query, keys, vals, scale):
    rows, cols, width = query.shape
    head_dim = width // HEADS
    query_h = query.reshape(rows, cols, HEADS, head_dim)
    key_piece = lax.all_gather(keys, "lon", axis=1, tiled=True).reshape(rows, -1, HEADS, head_dim)
    val_piece = lax.all_gather(vals, "lon", axis=1, tiled=True).reshape(rows, -1, HEADS, head_dim)
    scores = (
        jnp.einsum("aqhd,akhd->ahqk", query_h, key_piece, preferred_element_type=jnp.float32)
        * scale
    )
    expo = jnp.exp(scores)
    total = jnp.sum(expo, axis=-1)
    accum = jnp.einsum(
        "ahqk,akhd->ahqd", expo.astype(jnp.bfloat16), val_piece, preferred_element_type=jnp.float32
    )
    total, accum = (total, accum)
    summed = accum / total[..., None]
    return jnp.transpose(summed, (0, 2, 1, 3)).reshape(rows, cols, width).astype(jnp.bfloat16)


def body(fields, lat_mask, conv_first, conv_second, norm_gain, qkv_weight, out_weight):
    rows, cols, width = fields.shape
    mask_f = lat_mask.astype(jnp.float32)[:, None, None]
    scale = 1.0 / jnp.sqrt(jnp.float32(width // HEADS))
    state = (fields.astype(jnp.float32) * mask_f).astype(jnp.bfloat16)
    for blk in range(BLOCKS):
        hidden = (
            jax.nn.gelu(convolve(rims_single(state), conv_first[blk], 1, rows, cols)) * mask_f
        ).astype(jnp.bfloat16)
        second = jax.nn.gelu(convolve(rims_double(hidden), conv_second[blk], 2, rows, cols))
        mid = ((state.astype(jnp.float32) + second) * mask_f).astype(jnp.bfloat16)
        midf = mid.astype(jnp.float32)
        mean = jnp.mean(midf, axis=-1, keepdims=True)
        var = jnp.mean((midf - mean) ** 2, axis=-1, keepdims=True)
        normed = ((midf - mean) / jnp.sqrt(var + 1e-05) * norm_gain[blk]).astype(jnp.bfloat16)
        qkv = jnp.dot(normed, qkv_weight[blk], preferred_element_type=jnp.float32).astype(
            jnp.bfloat16
        )
        query = qkv[..., :width]
        keys = qkv[..., width : 2 * width]
        vals = qkv[..., 2 * width :]
        attended = attend_keys(query, keys, vals, scale)
        update = jnp.dot(attended, out_weight[blk], preferred_element_type=jnp.float32)
        state = ((midf + update) * mask_f).astype(jnp.bfloat16)
    return state


def solution(mesh):
    placed = (P("lat", "lon", None), P("lat"), P(), P(), P(), P(), P())
    return jax.shard_map(
        body, mesh=mesh, in_specs=placed, out_specs=P("lat", "lon", None), check_vma=False
    )
```

profile of v0, /device:TPU:1, one launch (start us, length us, event | category | flops | bytes accessed | tf_op | source)
XLA Modules:
  0.0 324.4 jit_solution(2557496878167897137)
XLA Ops:
  6.5 0.7 convert_element_type.70
  7.2 1.1 multiply_convert_fusion
  8.4 5.7 %collective-permute-start = (bf16[1,90,256]{2,1,0:T(8,128)(2,1)S(1)}, bf16[1,90,256]{2,1,0:T(8,128)(2,1)S(1)}, u32[]{:S(2)}, u32[]{:S(2)}) collective-permute-start(bf16[1,90,256]{2,1,0:T(8,128)(2,1)S(1)} %get-tuple-element.37), channel_id=1, source_target_pairs={{0,16},{16,32},{32,48},{48,64},{64,80},{80,96},{96,112},{112,128},... | collective-permute-start | bytes 138248 | tf_op jit(solution)/shard_map/ppermute | solution.py:18
  14.0 1.4 collective-permute-start.1
  15.5 2.0 slice_bitcast_fusion.1
  17.4 0.3 fusion.183
  18.0 0.5 copy-done.5
  18.5 2.0 collective-permute-done.1
  20.5 2.5 collective-permute-start.2
  23.5 0.3 collective-permute-done.2
  23.8 2.3 collective-permute-done.3
  26.6 0.3 fusion.160
  27.4 0.4 fusion.41
  27.8 0.6 fusion.66
  28.4 5.7 %collective-permute-start.4 = (bf16[2,90,256]{2,1,0:T(8,128)(2,1)S(1)}, bf16[2,90,256]{2,1,0:T(8,128)(2,1)S(1)}, u32[]{:S(2)}, u32[]{:S(2)}) collective-permute-start(bf16[2,90,256]{2,1,0:T(8,128)(2,1)S(1)} %get-tuple-element.35), channel_id=1, source_target_pairs={{0,16},{16,32},{32,48},{48,64},{64,80},{80,96},{96,112},{112,128},... | collective-permute-start | bytes 276488 | tf_op jit(solution)/shard_map/ppermute | solution.py:18
  34.1 1.3 collective-permute-start.5
  35.9 5.1 %collective-permute-done.5 = bf16[2,90,256]{2,1,0:T(8,128)(2,1)S(1)} collective-permute-done((bf16[2,90,256]{2,1,0:T(8,128)(2,1)S(1)}, bf16[2,90,256]{2,1,0:T(8,128)(2,1)S(1)}, u32[]{:S(2)}, u32[]{:S(2)}) %collective-permute-start.5) | collective-permute-done | bytes 92192 | tf_op jit(solution)/shard_map/ppermute | solution.py:20
  41.0 1.6 collective-permute-start.6
  42.6 0.4 collective-permute-start.7
  43.6 2.1 collective-permute-done.7
  46.2 0.3 fusion.150
  47.1 0.3 fusion.35
  47.4 0.8 convert_reduce_fusion.1
  48.2 0.4 fusion.55
  48.6 0.6 convolution_convert_fusion.1
  49.4 1.0 copy.30
  50.4 0.9 copy.32
  51.6 0.3 copy.29
  51.9 47.1 %all-gather.5.cloned.1.call-done = bf16[8,1440,256]{2,0,1:T(8,128)(2,1)} async-done(((bf16[8,90,256]{2,0,1:T(8,128)(2,1)}), bf16[8,1440,256]{2,0,1:T(8,128)(2,1)}) %all-gather.5.cloned.1.call-update) | async-done | bytes 5898256 | tf_op jit(solution)/shard_map/all_gather | solution.py:50
  99.0 9.1 %copy.31 = bf16[8,1440,256]{1,2,0:T(8,128)(2,1)} copy(bf16[8,1440,256]{2,0,1:T(8,128)(2,1)} %all-gather.5.cloned.1.call-done) | data formatting | bytes 11796480 | tf_op jit(solution)/shard_map/all_gather | solution.py:50
  108.1 12.6 %fusion = (f32[8,4,90]{2,1,0:T(4,128)S(1)}, f32[8,4,90,1440]{3,2,1,0:T(8,128)}) fusion(bf16[8,90,4,64]{1,3,2,0:T(8,128)(2,1)S(1)} %bitcast.245, bf16[8,1440,4,64]{1,3,2,0:T(8,128)(2,1)} %bitcast.241), kind=kOutput, calls=%fused_computation.2 | convolution fusion | flops 539133120 | bytes 22867200 | tf_op jit(solution)/shard_map/aqhd,akhd->ahqk/dot_general | solution.py:53
  120.6 24.1 %all-gather.7.cloned.1.call-done = bf16[8,1440,256]{2,0,1:T(8,128)(2,1)} async-done(((bf16[8,90,256]{2,0,1:T(8,128)(2,1)}), bf16[8,1440,256]{2,0,1:T(8,128)(2,1)}) %all-gather.7.cloned.1.call-update) | async-done | bytes 5898256 | tf_op jit(solution)/shard_map/all_gather | solution.py:51
  144.7 9.1 %copy.33 = bf16[8,1440,256]{1,2,0:T(8,128)(2,1)} copy(bf16[8,1440,256]{2,0,1:T(8,128)(2,1)} %all-gather.7.cloned.1.call-done) | data formatting | bytes 11796480 | tf_op jit(solution)/shard_map/all_gather | solution.py:51
  153.8 10.3 %divide_convert_fusion.1 = bf16[8,90,4,64]{1,3,2,0:T(8,128)(2,1)S(1)} fusion(bf16[8,1440,4,64]{1,3,2,0:T(8,128)(2,1)} %bitcast.239, f32[8,4,90,1440]{3,2,1,0:T(8,128)} %get-tuple-element.44, f32[8,90,4]{1,2,0:T(4,128)S(1)} %bitcast.247), kind=kOutput, calls=%fused_computation.65 | convolution fusion | flops 539504640 | bytes 22867200 | tf_op jit(solution)/shard_map/ahqk,akhd->ahqd/dot_general | solution.py:58
  164.1 0.3 fusion.43
  164.5 4.3 %collective-permute-start.8 = (bf16[1,90,256]{2,1,0:T(8,128)(2,1)S(1)}, bf16[1,90,256]{2,1,0:T(8,128)(2,1)S(1)}, u32[]{:S(2)}, u32[]{:S(2)}) collective-permute-start(bf16[1,90,256]{2,1,0:T(8,128)(2,1)S(1)} %get-tuple-element.33), channel_id=1, source_target_pairs={{0,16},{16,32},{32,48},{48,64},{64,80},{80,96},{96,112},{112,128},... | collective-permute-start | bytes 138248 | tf_op jit(solution)/shard_map/ppermute | solution.py:18
  168.8 1.3 collective-permute-start.9
  170.4 4.8 %collective-permute-done.9 = bf16[1,90,256]{2,1,0:T(8,128)(2,1)S(1)} collective-permute-done((bf16[1,90,256]{2,1,0:T(8,128)(2,1)S(1)}, bf16[1,90,256]{2,1,0:T(8,128)(2,1)S(1)}, u32[]{:S(2)}, u32[]{:S(2)}) %collective-permute-start.9) | collective-permute-done | bytes 46112 | tf_op jit(solution)/shard_map/ppermute | solution.py:20
  175.2 1.8 collective-permute-start.10
  177.8 2.3 collective-permute-done.11
  181.4 0.3 fusion.29
  181.7 0.6 fusion.85
  182.4 5.8 %collective-permute-start.12 = (bf16[2,90,256]{2,1,0:T(8,128)(2,1)S(1)}, bf16[2,90,256]{2,1,0:T(8,128)(2,1)S(1)}, u32[]{:S(2)}, u32[]{:S(2)}) collective-permute-start(bf16[2,90,256]{2,1,0:T(8,128)(2,1)S(1)} %get-tuple-element.31), channel_id=1, source_target_pairs={{0,16},{16,32},{32,48},{48,64},{64,80},{80,96},{96,112},{112,128},... | collective-permute-start | bytes 276488 | tf_op jit(solution)/shard_map/ppermute | solution.py:18
  188.2 1.3 collective-permute-start.13
  189.8 5.2 %collective-permute-done.13 = bf16[2,90,256]{2,1,0:T(8,128)(2,1)S(1)} collective-permute-done((bf16[2,90,256]{2,1,0:T(8,128)(2,1)S(1)}, bf16[2,90,256]{2,1,0:T(8,128)(2,1)S(1)}, u32[]{:S(2)}, u32[]{:S(2)}) %collective-permute-start.13) | collective-permute-done | bytes 92192 | tf_op jit(solution)/shard_map/ppermute | solution.py:20
  195.1 1.2 collective-permute-start.14
  196.3 1.2 collective-permute-start.15
  198.0 1.4 collective-permute-done.15
  200.2 0.3 fusion.137
  200.8 0.3 fusion.23
  201.1 0.8 convert_reduce_fusion
  201.9 0.4 fusion.52
  202.3 0.6 convolution_convert_fusion
  203.1 1.0 copy.36
  204.1 0.9 copy.38
  205.1 0.3 copy.35
  205.4 46.3 %all-gather.9.cloned.1.call-done = bf16[8,1440,256]{2,0,1:T(8,128)(2,1)} async-done(((bf16[8,90,256]{2,0,1:T(8,128)(2,1)}), bf16[8,1440,256]{2,0,1:T(8,128)(2,1)}) %all-gather.9.cloned.1.call-update) | async-done | bytes 5898256 | tf_op jit(solution)/shard_map/all_gather | solution.py:50
  251.7 9.1 %copy.37 = bf16[8,1440,256]{1,2,0:T(8,128)(2,1)} copy(bf16[8,1440,256]{2,0,1:T(8,128)(2,1)} %all-gather.9.cloned.1.call-done) | data formatting | bytes 11796480 | tf_op jit(solution)/shard_map/all_gather | solution.py:50
  260.8 12.6 %fusion.2 = (f32[8,4,90]{2,1,0:T(4,128)S(1)}, f32[8,4,90,1440]{3,2,1,0:T(8,128)}) fusion(bf16[8,90,4,64]{1,3,2,0:T(8,128)(2,1)S(1)} %bitcast.246, bf16[8,1440,4,64]{1,3,2,0:T(8,128)(2,1)} %bitcast.242), kind=kOutput, calls=%fused_computation.4 | convolution fusion | flops 539133120 | bytes 22867200 | tf_op jit(solution)/shard_map/aqhd,akhd->ahqk/dot_general | solution.py:53
  273.4 23.9 %all-gather.11.cloned.1.call-done = bf16[8,1440,256]{2,0,1:T(8,128)(2,1)} async-done(((bf16[8,90,256]{2,0,1:T(8,128)(2,1)}), bf16[8,1440,256]{2,0,1:T(8,128)(2,1)}) %all-gather.11.cloned.1.call-update) | async-done | bytes 5898256 | tf_op jit(solution)/shard_map/all_gather | solution.py:51
  297.3 9.1 %copy.39 = bf16[8,1440,256]{1,2,0:T(8,128)(2,1)} copy(bf16[8,1440,256]{2,0,1:T(8,128)(2,1)} %all-gather.11.cloned.1.call-done) | data formatting | bytes 11796480 | tf_op jit(solution)/shard_map/all_gather | solution.py:51
  306.4 10.2 %divide_convert_fusion = bf16[8,90,4,64]{1,3,2,0:T(8,128)(2,1)S(1)} fusion(bf16[8,1440,4,64]{1,3,2,0:T(8,128)(2,1)} %bitcast.240, f32[8,4,90,1440]{3,2,1,0:T(8,128)} %get-tuple-element.48, f32[8,90,4]{1,2,0:T(4,128)S(1)} %bitcast.248), kind=kOutput, calls=%fused_computation.64 | convolution fusion | flops 539504640 | bytes 22867200 | tf_op jit(solution)/shard_map/ahqk,akhd->ahqd/dot_general | solution.py:58
  316.6 0.3 fusion.42
  316.9 0.9 copy.41
  (76 shorter events, 8.9 us)
Async XLA Ops:
  6.5 92.5 %all-gather.5.cloned.1.call-start = ((), (), s32[]{:S(2)}) async-start(), calls=%async_computation | async-start | bytes 6266880 | tf_op jit(solution)/shard_map/all_gather | solution.py:50
  8.4 10.2 %collective-permute-start = (bf16[1,90,256]{2,1,0:T(8,128)(2,1)S(1)}, bf16[1,90,256]{2,1,0:T(8,128)(2,1)S(1)}, u32[]{:S(2)}, u32[]{:S(2)}) collective-permute-start(bf16[1,90,256]{2,1,0:T(8,128)(2,1)S(1)} %get-tuple-element.37), channel_id=1, source_target_pairs={{0,16},{16,32},{32,48},{48,64},{64,80},{80,96},{96,112},{112,128},... | collective-permute-start | bytes 138248 | tf_op jit(solution)/shard_map/ppermute | solution.py:18
  14.0 3.4 %copy-start.1 = (bf16[8,90,256]{2,0,1:T(8,128)(2,1)S(1)}, bf16[8,90,256]{2,0,1:T(8,128)(2,1)}, u32[]{:S(2)}) copy-start(bf16[8,90,256]{2,0,1:T(8,128)(2,1)} %param.7) | copy-start | bytes 1105924
  14.0 6.5 %collective-permute-start.1 = (bf16[1,90,256]{2,1,0:T(8,128)(2,1)S(1)}, bf16[1,90,256]{2,1,0:T(8,128)(2,1)S(1)}, u32[]{:S(2)}, u32[]{:S(2)}) collective-permute-start(bf16[1,90,256]{2,1,0:T(8,128)(2,1)S(1)} %get-tuple-element.38), channel_id=1, source_target_pairs={{16,0},{32,16},{48,32},{64,48},{80,64},{96,80},{112,96},{128,112},... | collective-permute-start | bytes 138248 | tf_op jit(solution)/shard_map/ppermute | solution.py:20
  15.5 2.4 copy-start
  17.8 0.7 copy-start.5
  20.5 3.3 %collective-permute-start.2 = (bf16[10,1,256]{2,1,0:T(2,128)(2,1)S(1)}, bf16[10,1,256]{2,1,0:T(2,128)(2,1)S(1)}, u32[]{:S(2)}, u32[]{:S(2)}) collective-permute-start(bf16[10,1,256]{2,1,0:T(2,128)(2,1)S(1)} %get-tuple-element.29), channel_id=1, source_target_pairs={{0,1},{1,2},{2,3},{3,4},{4,5},{5,6},{6,7},{7,8},{8,9},{9,10},{10,1... | collective-permute-start | bytes 15368 | tf_op jit(solution)/shard_map/ppermute | solution.py:18
  23.0 3.1 collective-permute-start.3
  28.4 7.5 %collective-permute-start.4 = (bf16[2,90,256]{2,1,0:T(8,128)(2,1)S(1)}, bf16[2,90,256]{2,1,0:T(8,128)(2,1)S(1)}, u32[]{:S(2)}, u32[]{:S(2)}) collective-permute-start(bf16[2,90,256]{2,1,0:T(8,128)(2,1)S(1)} %get-tuple-element.35), channel_id=1, source_target_pairs={{0,16},{16,32},{32,48},{48,64},{64,80},{80,96},{96,112},{112,128},... | collective-permute-start | bytes 276488 | tf_op jit(solution)/shard_map/ppermute | solution.py:18
  34.1 6.9 %collective-permute-start.5 = (bf16[2,90,256]{2,1,0:T(8,128)(2,1)S(1)}, bf16[2,90,256]{2,1,0:T(8,128)(2,1)S(1)}, u32[]{:S(2)}, u32[]{:S(2)}) collective-permute-start(bf16[2,90,256]{2,1,0:T(8,128)(2,1)S(1)} %get-tuple-element.36), channel_id=1, source_target_pairs={{16,0},{32,16},{48,32},{64,48},{80,64},{96,80},{112,96},{128,112},... | collective-permute-start | bytes 276488 | tf_op jit(solution)/shard_map/ppermute | solution.py:20
  41.0 2.5 collective-permute-start.6
  42.6 3.1 collective-permute-start.7
  47.4 1.2 copy-start.6
  48.2 1.0 copy-start.2
  50.4 94.4 %all-gather.7.cloned.1.call-start = ((), (), s32[]{:S(2)}) async-start(), calls=%async_computation.1 | async-start | bytes 6266880 | tf_op jit(solution)/shard_map/all_gather | solution.py:51
  51.4 200.3 %all-gather.9.cloned.1.call-start = ((), (), s32[]{:S(2)}) async-start(), calls=%async_computation.2 | async-start | bytes 6266880 | tf_op jit(solution)/shard_map/all_gather | solution.py:50
  153.8 10.3 %copy-start.3 = (bf16[8,90,256]{2,1,0:T(8,128)(2,1)S(1)}, bf16[8,90,256]{2,1,0:T(8,128)(2,1)}, u32[]{:S(2)}) copy-start(bf16[8,90,256]{2,1,0:T(8,128)(2,1)} %copy-done.2) | copy-start | bytes 1105924
  153.8 10.3 %copy-start.4 = (bf16[2,256,256]{2,1,0:T(8,128)(2,1)S(1)}, bf16[2,256,256]{2,1,0:T(8,128)(2,1)}, u32[]{:S(2)}) copy-start(bf16[2,256,256]{2,1,0:T(8,128)(2,1)} %param.13) | copy-start | bytes 786436
  164.5 5.9 %collective-permute-start.8 = (bf16[1,90,256]{2,1,0:T(8,128)(2,1)S(1)}, bf16[1,90,256]{2,1,0:T(8,128)(2,1)S(1)}, u32[]{:S(2)}, u32[]{:S(2)}) collective-permute-start(bf16[1,90,256]{2,1,0:T(8,128)(2,1)S(1)} %get-tuple-element.33), channel_id=1, source_target_pairs={{0,16},{16,32},{32,48},{48,64},{64,80},{80,96},{96,112},{112,128},... | collective-permute-start | bytes 138248 | tf_op jit(solution)/shard_map/ppermute | solution.py:18
  168.8 6.3 %collective-permute-start.9 = (bf16[1,90,256]{2,1,0:T(8,128)(2,1)S(1)}, bf16[1,90,256]{2,1,0:T(8,128)(2,1)S(1)}, u32[]{:S(2)}, u32[]{:S(2)}) collective-permute-start(bf16[1,90,256]{2,1,0:T(8,128)(2,1)S(1)} %get-tuple-element.34), channel_id=1, source_target_pairs={{16,0},{32,16},{48,32},{64,48},{80,64},{96,80},{112,96},{128,112},... | collective-permute-start | bytes 138248 | tf_op jit(solution)/shard_map/ppermute | solution.py:20
  175.2 2.7 collective-permute-start.10
  177.0 3.1 collective-permute-start.11
  182.4 7.5 %collective-permute-start.12 = (bf16[2,90,256]{2,1,0:T(8,128)(2,1)S(1)}, bf16[2,90,256]{2,1,0:T(8,128)(2,1)S(1)}, u32[]{:S(2)}, u32[]{:S(2)}) collective-permute-start(bf16[2,90,256]{2,1,0:T(8,128)(2,1)S(1)} %get-tuple-element.31), channel_id=1, source_target_pairs={{0,16},{16,32},{32,48},{48,64},{64,80},{80,96},{96,112},{112,128},... | collective-permute-start | bytes 276488 | tf_op jit(solution)/shard_map/ppermute | solution.py:18
  188.2 6.9 %collective-permute-start.13 = (bf16[2,90,256]{2,1,0:T(8,128)(2,1)S(1)}, bf16[2,90,256]{2,1,0:T(8,128)(2,1)S(1)}, u32[]{:S(2)}, u32[]{:S(2)}) collective-permute-start(bf16[2,90,256]{2,1,0:T(8,128)(2,1)S(1)} %get-tuple-element.32), channel_id=1, source_target_pairs={{16,0},{32,16},{48,32},{64,48},{80,64},{96,80},{112,96},{128,112},... | collective-permute-start | bytes 276488 | tf_op jit(solution)/shard_map/ppermute | solution.py:20
  195.1 2.9 collective-permute-start.14
  196.3 3.1 collective-permute-start.15
  201.1 1.2 copy-start.7
  204.1 93.2 %all-gather.11.cloned.1.call-start = ((), (), s32[]{:S(2)}) async-start(), calls=%async_computation.3 | async-start | bytes 6266880 | tf_op jit(solution)/shard_map/all_gather | solution.py:51
Sparse Core Ops, SparseCore 0:
  50.5 48.4 all-gather.4
  100.8 43.8 all-gather.6
  204.2 47.4 all-gather.8
  253.4 43.8 all-gather.10
where the time goes:
time: 326 us; the launch traced here: 324 us
  waiting for transfers between devices  168 us (52%)
  matrix products  59.1 us (18%)
  local copies, waits for them, and re-layouts  44.7 us (14%)
  starting transfers between devices  35.8 us (11%)
  between operations  13.7 us (4%)
  other arithmetic  3.56 us (1%)
    all_gather x2, waiting for transfers between devices, attend_keys(): lax.all_gather(keys, 'lon', axis=1, tiled=True)  93.4 us
    all_gather x2, waiting for transfers between devices, attend_keys(): lax.all_gather(vals, 'lon', axis=1, tiled=True)  48.1 us
    ppermute x8, starting transfers between devices, padded_2(): lax.ppermute(tail, axis, [(i, (i + 1) % count) for i in range(ends)])  28.6 us
    ppermute x8, waiting for transfers between devices, padded_2(): lax.ppermute(head, axis, [((i + 1) % count, i) for i in range(ends)])  25.2 us
    dot_general x2, matrix products, attend_keys(): jnp.einsum('aqhd,akhd->ahqk', query_h, key_piece, preferred_element_type=...  25.1 us
    dot_general x2, matrix products, attend_keys(): jnp.einsum('ahqk,akhd->ahqd', expo.astype(jnp.bfloat16), val_piece, prefe...  20.4 us
    all_gather x2, local copies, waits for them, and re-layouts, attend_keys(): lax.all_gather(vals, 'lon', axis=1, tiled=True)  18.1 us
    all_gather x2, local copies, waits for them, and re-layouts, attend_keys(): lax.all_gather(keys, 'lon', axis=1, tiled=True)  18.1 us
  transfers between devices with their start and end apart: 20, of which 16 were waited for; matrix products, arithmetic and copies ran while one was open for 16% of the time, Pallas kernels for 0%

commit v1 on v0

v1 whole, which is shorter than its diff:
```python
import math

import jax
import jax.numpy as jnp
from jax import lax
from jax.experimental import pallas as pl
from jax.experimental.pallas import tpu as pltpu
from jax.sharding import PartitionSpec as P

HEADS = 4
BLOCKS = 2
EDGE = 3
CORES = 2
BF = jnp.bfloat16
F32 = jnp.float32
MESH = pl.DeviceIdType.MESH


def conv(src, start, count, spread, weights):
    wide, width = src.shape[1], src.shape[2]
    cells = count * wide
    taps = [src[pl.ds(start + i * spread, count)].reshape(cells, width) for i in range(3)]
    lhs = jnp.concatenate(taps, axis=1)
    parts = [
        jnp.dot(lhs, weights[:, j].reshape(3 * width, width), preferred_element_type=F32)
        for j in range(3)
    ]
    return pltpu.roll(parts[0], spread, 0) + parts[1] + pltpu.roll(parts[2], cells - spread, 0)


def kernel(
    fields, mask, w1_hbm, w2_hbm, gain, wqkv_hbm, wo_hbm, out,
    w1, w2, wqkv, wo, xs, xb, hb, mb, midb, epack, erecv, nself, nbuf, qb, kb, vx, att, abuf,
    wsem, e_send, e_recv, l_send, l_recv, m_sem, f_send, f_recv, s_send, s_recv, r_send, r_recv,
):
    rows, cols, width = fields.shape
    wide = cols + 2 * EDGE
    head_dim = width // HEADS
    lats, lons = lax.axis_size("lat"), lax.axis_size("lon")
    chips = lons // CORES
    groups = chips // 2
    half = chips * wide
    lat, lon = lax.axis_index("lat"), lax.axis_index("lon")
    chip, core = lon // CORES, lon % CORES
    group = chip // 2
    up, down = (lat + lats - 1) % lats, (lat + 1) % lats
    left, right = (lon + lons - 1) % lons, (lon + 1) % lons
    sibling = chip * CORES + 1 - core
    beyond = (lon + lons - 1 + 2 * core) % lons

    def remote(src, dst, send, recv, to):
        return pltpu.make_async_remote_copy(
            src_ref=src, dst_ref=dst, send_sem=send, recv_sem=recv, device_id=to, device_id_type=MESH
        )

    def each(count, body):
        lax.fori_loop(0, count, lambda k, carry: (body(k), carry)[1], 0)

    barrier = pltpu.get_barrier_semaphore()

    def greet(to):
        pl.semaphore_signal(barrier, inc=1, device_id=to, device_id_type=MESH)

    greet((up, lon))
    greet((down, lon))
    greet((lat, sibling))
    greet((lat, beyond))
    each(chips - 1, lambda k: greet((lat, (chip + 1 + k) % chips * CORES + core)))

    def weight_copies(blk):
        return [
            pltpu.make_async_copy(w1_hbm.at[blk], w1.at[blk], wsem.at[0, blk]),
            pltpu.make_async_copy(w2_hbm.at[blk], w2.at[blk], wsem.at[1, blk]),
            pltpu.make_async_copy(wqkv_hbm.at[blk], wqkv.at[blk], wsem.at[2, blk]),
            pltpu.make_async_copy(wo_hbm.at[blk], wo.at[blk], wsem.at[3, blk]),
        ]

    for blk in range(BLOCKS):
        for copy in weight_copies(blk):
            copy.start()

    xs[...] = jnp.zeros_like(xs)
    for a in range(rows):
        on = mask[a].astype(F32)
        mb[EDGE + a] = jnp.full(mb.shape[1:], on, F32)
        xs[a, EDGE : EDGE + cols, :] = fields[a].astype(F32) * on
    xb[0, EDGE : EDGE + rows] = xs[...].astype(BF)
    mb[0:EDGE] = jnp.full((EDGE,) + mb.shape[1:], jnp.where(lat > 0, 1.0, 0.0), F32)

    pl.semaphore_wait(barrier, chips + 3)

    def mask_copy():
        return remote(
            mb.at[pl.ds(EDGE, EDGE)], mb.at[pl.ds(EDGE + rows, EDGE)], m_sem.at[0], m_sem.at[1], (up, lon)
        )

    mask_copy().start()

    def row_mask(first, count):
        on = mb[pl.ds(first, count)][:, :1, :]
        return jnp.concatenate([on, on], axis=2)

    column = lax.broadcasted_iota(jnp.int32, (1, wide, 1), 1)
    inside = (column >= EDGE) & (column < EDGE + cols)

    def block(blk):
        x = xb.at[blk]
        own = pl.ds(EDGE, rows)
        w1_copy, w2_copy, wqkv_copy, wo_copy = weight_copies(blk)

        low = x[own, 0:16, :].astype(F32)
        high = x[own, wide - 16 : wide, :].astype(F32)
        epack[blk, 0] = pltpu.roll(low[:, 0:8], 2, 1).reshape(rows * 8, width).astype(BF)
        epack[blk, 1] = pltpu.roll(high[:, 8:16], 6, 1).reshape(rows * 8, width).astype(BF)

        def edge_copies():
            return [
                remote(epack.at[blk, 0], erecv.at[blk, 1], e_send.at[blk, 0], e_recv.at[blk, 1], (lat, left)),
                remote(epack.at[blk, 1], erecv.at[blk, 0], e_send.at[blk, 1], e_recv.at[blk, 0], (lat, right)),
            ]

        for copy in edge_copies():
            copy.start()
        for copy in edge_copies():
            copy.wait_recv()
        place = lax.broadcasted_iota(jnp.int32, (rows, 16, width), 1)
        nothing = jnp.zeros((rows, 8, width), F32)
        from_left = erecv[blk, 0].astype(F32).reshape(rows, 8, width)
        from_right = erecv[blk, 1].astype(F32).reshape(rows, 8, width)
        x[own, 0:16, :] = jnp.where(
            place < EDGE, jnp.concatenate([from_left, nothing], axis=1), low
        ).astype(BF)
        x[own, wide - 16 : wide, :] = jnp.where(
            place >= 16 - EDGE, jnp.concatenate([nothing, from_right], axis=1), high
        ).astype(BF)

        def row_copies():
            top, bottom = pl.ds(EDGE, EDGE), pl.ds(rows, EDGE)
            above, below = pl.ds(0, EDGE), pl.ds(EDGE + rows, EDGE)
            return [
                remote(x.at[top], x.at[below], l_send.at[blk, 0], l_recv.at[blk, 1], (up, lon)),
                remote(x.at[bottom], x.at[above], l_send.at[blk, 1], l_recv.at[blk, 0], (down, lon)),
            ]

        for copy in row_copies():
            copy.start()

        w1_copy.wait()

        def first(start):
            got = conv(x, start, EDGE, 1, w1.at[blk])
            got = jax.nn.gelu(got).reshape(EDGE, wide, width) * row_mask(start + 1, EDGE)
            hb[pl.ds(start, EDGE)] = got.astype(BF)

        each(2, lambda k: first(EDGE * (1 + k)))
        for copy in row_copies():
            copy.wait_recv()

        @pl.when(blk == 0)
        def _():
            mask_copy().wait_recv()

        @pl.when(lat == 0)
        def _():
            x[0:EDGE] = jnp.zeros((EDGE, wide, width), BF)

        @pl.when(lat == lats - 1)
        def _():
            x[EDGE + rows :] = jnp.zeros((EDGE, wide, width), BF)
            mb[EDGE + rows :] = jnp.zeros((EDGE,) + mb.shape[1:], F32)

        each(2, lambda k: first(3 * EDGE * k))

        w2_copy.wait()

        def row_copy(r, to):
            return remote(
                nself.at[blk, r], nbuf.at[blk, core, chip], f_send.at[blk, r], f_recv.at[blk, chip],
                (lat, to * CORES + core),
            )

        def second(k):
            pair = (group + 1 + k) % groups
            a = pair * 2
            got = jax.nn.gelu(conv(hb, a, 2, 2, w2.at[blk])).reshape(2, wide, width)
            got = (x[pl.ds(a + EDGE, 2)].astype(F32) + got) * row_mask(a + EDGE, 2)
            got = got.astype(BF)
            midb[pl.ds(a, 2)] = got
            got = got.astype(F32)
            got = got - jnp.mean(got, axis=-1, keepdims=True)
            var = jnp.mean(got * got, axis=-1, keepdims=True)
            got = got * lax.rsqrt(var + 1e-05) * gain[blk]
            nself[blk, pl.ds(a, 2)] = jnp.where(inside, got, 0.0).astype(BF)
            for i in range(2):
                r = a + i

                @pl.when(r != chip)
                def _():
                    row_copy(r, r).start()

                @pl.when(r == chip)
                def _():
                    nbuf[blk, core, r] = nself[blk, r]

        each(groups, second)

        def half_copy(source):
            slot = nbuf.at[blk, core, source]
            return remote(slot, slot, s_send.at[blk, source], s_recv.at[blk, source], (lat, sibling))

        def pass_on(k):
            source = ((group + 2 * groups - 1 - k // 2) % groups) * 2 + k % 2

            @pl.when(source != chip)
            def _():
                remote(
                    nself.at[blk, source], nbuf.at[blk, core, source], f_send.at[blk, source],
                    f_recv.at[blk, source], (lat, source * CORES + core),
                ).wait_recv()

            half_copy(source).start()

        each(chips, pass_on)

        wqkv_copy.wait()
        mine = nbuf[blk, core].reshape(half, width)
        scale = math.log2(math.e) / math.sqrt(head_dim)
        query = jnp.dot(mine, wqkv[blk, :, 0:width], preferred_element_type=F32) * scale
        qb[...] = query.astype(BF).reshape(chips, wide, width)
        lane = lax.broadcasted_iota(jnp.int32, (1, 1, 2 * head_dim), 2)
        first_head = lane < head_dim
        ones = jnp.where(inside, 1.0, 0.0)

        def keys_values(t):
            side = (core + t) % CORES

            @pl.when(t == 1)
            def _():
                each(chips, lambda source: half_copy(source).wait_recv())

            cells = nbuf[blk, side].reshape(half, width)
            both = jnp.dot(cells, wqkv[blk, :, width:], preferred_element_type=F32)
            kb[side] = both[:, :width].astype(BF)
            values = both[:, width:].reshape(chips, wide, width)
            for h in range(HEADS):
                pair = values[:, :, h // 2 * 2 * head_dim :][:, :, : 2 * head_dim]
                keep = first_head if h % 2 == 0 else ~first_head
                vx[h, side] = jnp.where(keep, pair, ones).astype(BF).reshape(half, 2 * head_dim)

        each(CORES, keys_values)

        def back_copy(slot, row, to):
            return remote(
                att.at[blk, slot], abuf.at[blk, row], r_send.at[blk, slot], r_recv.at[blk, row],
                (lat, to * CORES + core),
            )

        def attend(k):
            pair = (group + 1 + k) % groups
            a = pair * 2
            query = qb[pl.ds(a, 2)].reshape(2 * wide, width)
            low_lane = lax.broadcasted_iota(jnp.int32, (1, 2 * head_dim), 1) < head_dim
            zero = jnp.zeros((), BF)
            for p in range(HEADS // 2):
                span = slice(p * 2 * head_dim, (p + 1) * 2 * head_dim)
                both = query[:, span]
                lhs = jnp.concatenate(
                    [jnp.where(low_lane, both, zero), jnp.where(low_lane, zero, both)], axis=0
                )
                keys = kb[:, :, span].reshape(CORES * half, 2 * head_dim)
                scores = lax.dot_general(
                    lhs, keys, (((1,), (1,)), ((), ())), preferred_element_type=F32
                )
                expo = jnp.exp2(scores).astype(BF)
                got = []
                for e in range(2):
                    values = vx[2 * p + e].reshape(CORES * half, 2 * head_dim)
                    part = jnp.dot(
                        expo[e * 2 * wide : (e + 1) * 2 * wide], values, preferred_element_type=F32
                    )
                    got.append(part / pltpu.roll(part, head_dim, 1))
                done = jnp.where(low_lane, got[0], got[1]).astype(BF)
                att[blk, pl.ds(a, 2), :, span] = done.reshape(2, wide, 2 * head_dim)
            for i in range(2):
                home = a + i

                @pl.when(home != chip)
                def _():
                    back_copy(home, chip, home).start()

                @pl.when(home == chip)
                def _():
                    abuf[blk, home] = att[blk, home]

        each(groups, attend)

        wo_copy.wait()

        def arrived(k):
            row = (chip + 1 + k) % chips
            back_copy(row, row, row).wait_recv()

        each(chips - 1, arrived)

        def project(k):
            a = k * 2
            cells = abuf[blk, pl.ds(a, 2)].reshape(2 * wide, width)
            got = jnp.dot(cells, wo[blk], preferred_element_type=F32).reshape(2, wide, width)
            got = (midb[pl.ds(a, 2)].astype(F32) + got) * row_mask(a + EDGE, 2)
            xb[blk + 1, pl.ds(a + EDGE, 2)] = got.astype(BF)

        each(rows // 2, project)

        for copy in edge_copies() + row_copies():
            copy.wait_send()

        def left_here(k):
            to = (chip + 1 + k) % chips
            row_copy(to, to).wait_send()
            back_copy(to, chip, to).wait_send()

        each(chips - 1, left_here)
        each(chips, lambda source: half_copy(source).wait_send())

    each(BLOCKS, block)
    mask_copy().wait_send()
    out[...] = xb[BLOCKS, EDGE : EDGE + rows]


def body(fields, lat_mask, conv_first, conv_second, norm_gain, qkv_weight, out_weight):
    rows, cols, width = fields.shape
    wide = cols + 2 * EDGE
    chips = lax.axis_size("lon") // CORES
    half = chips * wide
    head_dim = width // HEADS
    vmem = pl.BlockSpec(memory_space=pltpu.VMEM)
    hbm = pl.BlockSpec(memory_space=pl.ANY)
    dma = pltpu.SemaphoreType.DMA
    wide_out = pl.pallas_call(
        kernel,
        out_shape=jax.ShapeDtypeStruct((rows, wide, width), BF),
        in_specs=[vmem, pl.BlockSpec(memory_space=pltpu.SMEM), hbm, hbm, vmem, hbm, hbm],
        out_specs=vmem,
        scratch_shapes=[
            pltpu.VMEM(conv_first.shape, BF),
            pltpu.VMEM(conv_second.shape, BF),
            pltpu.VMEM(qkv_weight.shape, BF),
            pltpu.VMEM(out_weight.shape, BF),
            pltpu.VMEM((rows, wide, width), F32),
            pltpu.VMEM((BLOCKS + 1, rows + 2 * EDGE, wide, width), BF),
            pltpu.VMEM((rows + 4, wide, width), BF),
            pltpu.VMEM((rows + 2 * EDGE, 8, width // 2), F32),
            pltpu.VMEM((rows, wide, width), BF),
            pltpu.VMEM((BLOCKS, 2, rows * 8, width), BF),
            pltpu.VMEM((BLOCKS, 2, rows * 8, width), BF),
            pltpu.VMEM((BLOCKS, rows, wide, width), BF),
            pltpu.VMEM((BLOCKS, CORES, chips, wide, width), BF),
            pltpu.VMEM((chips, wide, width), BF),
            pltpu.VMEM((CORES, half, width), BF),
            pltpu.VMEM((HEADS, CORES, half, 2 * head_dim), BF),
            pltpu.VMEM((BLOCKS, chips, wide, width), BF),
            pltpu.VMEM((BLOCKS, rows, wide, width), BF),
            dma((4, BLOCKS)),
            dma((BLOCKS, 2)),
            dma((BLOCKS, 2)),
            dma((BLOCKS, 2)),
            dma((BLOCKS, 2)),
            dma((2,)),
            dma((BLOCKS, chips)),
            dma((BLOCKS, chips)),
            dma((BLOCKS, chips)),
            dma((BLOCKS, chips)),
            dma((BLOCKS, chips)),
            dma((BLOCKS, chips)),
        ],
        compiler_params=pltpu.CompilerParams(
            collective_id=0, has_side_effects=True, vmem_limit_bytes=50 * 1024 * 1024
        ),
    )(
        fields,
        lat_mask,
        conv_first,
        conv_second,
        norm_gain.reshape(BLOCKS, 1, width),
        qkv_weight,
        out_weight,
    )
    return wide_out[:, EDGE : EDGE + cols]


def solution(mesh):
    placed = (P("lat", "lon", None), P("lat"), P(), P(), P(), P(), P())
    return jax.shard_map(
        body, mesh=mesh, in_specs=placed, out_specs=P("lat", "lon", None), check_vma=False
    )
```

time: 326 us -> 83.1 us (0.25)
  waiting for transfers between devices: 168 us -> 0 us
  Pallas kernels: 0 us -> 77.4 us
  matrix products: 59.1 us -> 0 us
  local copies, waits for them, and re-layouts: 44.7 us -> 5.51 us
  starting transfers between devices: 35.8 us -> 0 us
  between operations: 13.7 us -> 0.03 us
  other arithmetic: 3.56 us -> 0 us
    all_gather x4 -> x0, waiting for transfers between devices: 141 us -> none  [the longest x2 93.4 us: attend_keys(): lax.all_gather(keys, 'lon', axis=1, tiled=True)]
    pallas_call x0 -> x1, Pallas kernels: none -> 77.4 us  [body(): pl.pallas_call(kernel, out_shape=jax.ShapeDtypeStruct((rows, wide, width)...]
    dot_general x44 -> x0, matrix products: 59.1 us -> none  [the longest x2 25.1 us: attend_keys(): jnp.einsum('aqhd,akhd->ahqk', query_h, key_piece, preferred_element_type=...]
    all_gather x4 -> x0, local copies, waits for them, and re-layouts: 36.3 us -> none  [the longest x2 18.1 us: attend_keys(): lax.all_gather(vals, 'lon', axis=1, tiled=True)]
    ppermute x16 -> x0, starting transfers between devices: 35.5 us -> none  [the longest x8 28.6 us: padded_2(): lax.ppermute(tail, axis, [(i, (i + 1) % count) for i in range(ends)])]
    ppermute x16 -> x0, waiting for transfers between devices: 26.1 us -> none  [the longest x8 25.2 us: padded_2(): lax.ppermute(head, axis, [((i + 1) % count, i) for i in range(ends)])]
    slice x13 -> x2, local copies, waits for them, and re-layouts: 4.75 us -> 1.04 us  [body(): return wide_out[:, EDGE:EDGE + cols]]
  transfers between devices with their start and end apart: 20 -> 0, of which waited for: 16 -> 0; matrix products, arithmetic and copies ran while one was open for 16% -> 0% of each run, Pallas kernels for 0% -> 0%
where the time goes in v1:
time: 83.1 us; the launch traced here: 82.9 us
  Pallas kernels  77.4 us (93%)
  local copies, waits for them, and re-layouts  5.51 us (7%)
    pallas_call x1, Pallas kernels, body(): pl.pallas_call(kernel, out_shape=jax.ShapeDtypeStruct((rows, wide, width)...  77.4 us
    unnamed x7, local copies, waits for them, and re-layouts  3.79 us

profile of v1, /device:TPU:1, one launch (start us, length us, event | category | flops | bytes accessed | tf_op | source)
XLA Modules:
  0.0 82.9 jit_solution(4890152556324709727)
XLA Ops:
  0.0 0.7 reshape.3.gain
  0.7 1.1 %copy.8.fields = bf16[8,90,256]{2,1,0:T(8,128)(2,1)S(1)} copy(bf16[8,90,256]{2,0,1:T(8,128)(2,1)} %param.7) | data formatting | bytes 737280 | tf_op args[0]
  1.7 0.0 copy-start
  1.8 1.1 %copy-done = bf16[2,256,768]{2,1,0:T(8,128)(2,1)S(1)} copy-done((bf16[2,256,768]{2,1,0:T(8,128)(2,1)S(1)}, bf16[2,256,768]{2,1,0:T(8,128)(2,1)}, u32[]{:S(2)}) %copy-start) | copy-done | bytes 786456
  2.9 0.0 copy-start.1
  2.9 0.9 %copy-done.1 = bf16[2,256,256]{2,1,0:T(8,128)(2,1)S(1)} copy-done((bf16[2,256,256]{2,1,0:T(8,128)(2,1)S(1)}, bf16[2,256,256]{2,1,0:T(8,128)(2,1)}, u32[]{:S(2)}) %copy-start.1) | copy-done | bytes 262168
  3.8 0.0 copy-start.2
  3.8 0.7 copy-done.2
  4.5 77.4 %shard_map.73 = bf16[8,96,256]{2,1,0:T(8,128)(2,1)S(1)} custom-call(bf16[8,90,256]{2,1,0:T(8,128)(2,1)S(1)} %copy.8.fields, s32[8]{0:T(128)S(1)} %copy-done.2, bf16[2,3,3,256,256]{4,3,2,1,0:T(8,128)(2,1)} %w1_hbm.1, bf16[2,3,3,256,256]{4,3,2,1,0:T(8,128)(2,1)} %w2_hbm.1, f32[2,1,256]{2,1,0:T(1,128)S(1)} %reshape.3.gain, bf16[2,256,768]{2,1,0:T(8,128)(2,1)S(1)} %copy-done, ...), custom_call_target="tpu_custom_call" | custom-call | tf_op jit(solution)/shard_map/pallas_call | solution.py:339
  81.9 0.1 slice.3
  82.0 0.9 %copy.9 = bf16[8,90,256]{2,0,1:T(8,128)(2,1)} copy(bf16[8,90,256]{2,1,0:T(8,128)(2,1)S(1)} %slice.3) | data formatting | bytes 737280 | tf_op jit(solution)/shard_map/slice | solution.py:388
Async XLA Ops:
  1.7 1.1 %copy-start = (bf16[2,256,768]{2,1,0:T(8,128)(2,1)S(1)}, bf16[2,256,768]{2,1,0:T(8,128)(2,1)}, u32[]{:S(2)}) copy-start(bf16[2,256,768]{2,1,0:T(8,128)(2,1)} %wqkv_hbm.1) | copy-start | bytes 2359300
  2.9 0.9 %copy-start.1 = (bf16[2,256,256]{2,1,0:T(8,128)(2,1)S(1)}, bf16[2,256,256]{2,1,0:T(8,128)(2,1)}, u32[]{:S(2)}) copy-start(bf16[2,256,256]{2,1,0:T(8,128)(2,1)} %wo_hbm.1) | copy-start | bytes 786436
  3.8 0.7 copy-start.2

commit v2 on v1

v2 whole, which is shorter than its diff:
```python
import math

import jax
import jax.numpy as jnp
from jax import lax
from jax.experimental import pallas as pl
from jax.experimental.pallas import tpu as pltpu
from jax.sharding import PartitionSpec as P

HEADS = 4
BLOCKS = 2
EDGE = 3
CORES = 2
RING = 4
BF = jnp.bfloat16
F32 = jnp.float32
MESH = pl.DeviceIdType.MESH


def conv(src, start, count, spread, weights):
    wide, width = src.shape[1], src.shape[2]
    cells = count * wide
    taps = [src[pl.ds(start + i * spread, count)].reshape(cells, width) for i in range(3)]
    lhs = jnp.concatenate(taps, axis=1)
    parts = [
        jnp.dot(lhs, weights[:, j].reshape(3 * width, width), preferred_element_type=F32)
        for j in range(3)
    ]
    return pltpu.roll(parts[0], spread, 0) + parts[1] + pltpu.roll(parts[2], cells - spread, 0)


def shifted(cells, start, by):
    tile = cells[:, start // 16 * 16 : start // 16 * 16 + 16, :].astype(F32)
    return pltpu.roll(tile[:, start % 16 : start % 16 + 8], by, 1)


def with_edges(ref, index, from_left, from_right):
    count, _, width = from_left.shape
    wide = ref.shape[-2]
    place = lax.broadcasted_iota(jnp.int32, (count, 16, width), 1)
    nothing = jnp.zeros(from_left.shape, F32)
    low = ref[index, 0:16, :].astype(F32)
    high = ref[index, wide - 16 : wide, :].astype(F32)
    ref[index, 0:16, :] = jnp.where(
        place < EDGE, jnp.concatenate([from_left, nothing], axis=1), low
    ).astype(BF)
    ref[index, wide - 16 : wide, :] = jnp.where(
        place >= 16 - EDGE, jnp.concatenate([nothing, from_right], axis=1), high
    ).astype(BF)


def kernel(
    fields, mask, w1_hbm, w2_hbm, gain, wqkv_hbm, wo_hbm, out,
    w1, w2, wqkv, wo, xs, xb, hb, mp, epack, erecv, nself, nbuf, qm, kb, vx, att,
    wsem, e_send, e_recv, l_send, l_recv, m_sem, f_send, f_recv, s_send, s_recv, h_send, n_send, x_recv,
):
    rows, cols, width = fields.shape
    wide = cols + 2 * EDGE
    head_dim = width // HEADS
    lats, lons = lax.axis_size("lat"), lax.axis_size("lon")
    chips = lons // CORES
    groups = chips // 2
    half = chips * wide
    lat, lon = lax.axis_index("lat"), lax.axis_index("lon")
    chip, core = lon // CORES, lon % CORES
    z, y_hi = lat // 2, lat % 2
    x_at, y_at = lon // 4, y_hi * 2 + (lon // 2) % 2
    up, down = (lat + lats - 1) % lats, (lat + 1) % lats
    left, right = (lon + lons - 1) % lons, (lon + 1) % lons
    sibling = chip * CORES + 1 - core
    band_1, sector_1 = z * 2 + core, x_at * 4 + (y_at + x_at) % RING

    def place_1(band, sector):
        x = sector // 4
        y = (sector + 3 * x) % RING
        return band // 2 * 2 + y // 2, x * 4 + y % 2 * 2 + band % 2

    def placed(blk, band, sector):
        there = place_1(band, sector)
        return band + blk * (there[0] - band), sector + blk * (there[1] - sector)

    def elsewhere(to):
        return (to[0] != lat) | (to[1] != lon)

    def remote(src, dst, send, recv, to):
        return pltpu.make_async_remote_copy(
            src_ref=src, dst_ref=dst, send_sem=send, recv_sem=recv, device_id=to, device_id_type=MESH
        )

    def each(count, body):
        lax.fori_loop(0, count, lambda k, carry: (body(k), carry)[1], 0)

    def across(k):
        return (x_at + 2 - k + k // 2 * (2 * k - 1) + RING) % RING

    barrier = pltpu.get_barrier_semaphore()

    def greet(to):
        @pl.when(elsewhere(to))
        def _():
            pl.semaphore_signal(barrier, inc=1, device_id=to, device_id_type=MESH)

    def count(to):
        return jnp.where(elsewhere(to), 1, 0)

    def row_at(place):
        row = place - EDGE + rows
        return (band_1 + row // rows - 1 + lats) % lats, row % rows * CORES + sector_1 % 2

    beside = (lat + lats + chip // 5 - (7 - chip) // 5) % lats
    is_halo = (chip < EDGE) | (chip >= rows - EDGE)

    for to in ((up, lon), (down, lon), (lat, left), (lat, right), (lat, sibling)):
        greet(to)
    each(chips, lambda i: greet((lat, i * CORES + core)))
    each(chips, lambda i: greet(place_1(lat, i * CORES + core)))
    each(rows + 2 * EDGE, lambda place: greet(row_at(place)))

    def weight_copies(blk):
        return [
            pltpu.make_async_copy(w1_hbm.at[blk], w1.at[blk], wsem.at[0, blk]),
            pltpu.make_async_copy(w2_hbm.at[blk], w2.at[blk], wsem.at[1, blk]),
            pltpu.make_async_copy(wqkv_hbm.at[blk], wqkv.at[blk], wsem.at[2, blk]),
            pltpu.make_async_copy(wo_hbm.at[blk], wo.at[blk], wsem.at[3, blk]),
        ]

    for blk in range(BLOCKS):
        for copy in weight_copies(blk):
            copy.start()

    xs[...] = jnp.zeros_like(xs)
    for a in range(rows):
        on = mask[a].astype(F32)
        mp[EDGE + y_hi * rows + a] = jnp.full(mp.shape[1:], on, F32)
        xs[a, EDGE : EDGE + cols, :] = fields[a].astype(F32) * on
    own = pl.ds(EDGE, rows)
    xb[0, own] = xs[...].astype(BF)
    mp[0:EDGE] = jnp.full((EDGE,) + mp.shape[1:], jnp.where(z > 0, 1.0, 0.0), F32)
    mp[EDGE + 2 * rows :] = jnp.full((EDGE,) + mp.shape[1:], jnp.where(z < lats // 2 - 1, 1.0, 0.0), F32)
    epack[0] = shifted(xb[0, own], 0, 2).reshape(rows * 8, width).astype(BF)
    epack[1] = shifted(xb[0, own], wide - 8, 6).reshape(rows * 8, width).astype(BF)

    heard = 5
    for i in range(chips):
        heard += count((lat, i * CORES + core)) + count(place_1(lat, i * CORES + core))
        heard += count((band_1, i * CORES + sector_1 % 2))
        heard += jnp.where(is_halo, count(place_1(beside, i * CORES + core)), 0)
    pl.semaphore_wait(barrier, heard)

    def mask_copy():
        both = mp.at[pl.ds(EDGE + y_hi * rows, rows)]
        return remote(both, both, m_sem.at[0], m_sem.at[1], (lat + 1 - 2 * y_hi, lon))

    def edge_copies():
        return [
            remote(epack.at[0], erecv.at[1], e_send.at[0], e_recv.at[1], (lat, left)),
            remote(epack.at[1], erecv.at[0], e_send.at[1], e_recv.at[0], (lat, right)),
        ]

    def row_copies(n):
        columns = (pl.ds(16, wide - 32), pl.ds(0, 16), pl.ds(wide - 16, 16))[n]
        top, bottom = xb.at[0, pl.ds(EDGE, EDGE), columns], xb.at[0, pl.ds(rows, EDGE), columns]
        above, below = xb.at[0, pl.ds(0, EDGE), columns], xb.at[0, pl.ds(EDGE + rows, EDGE), columns]
        return [
            remote(top, below, l_send.at[n, 0], l_recv.at[n, 1], (up, lon)),
            remote(bottom, above, l_send.at[n, 1], l_recv.at[n, 0], (down, lon)),
        ]

    for copy in edge_copies() + row_copies(0):
        copy.start()
    mask_copy().start()

    for copy in edge_copies():
        copy.wait_recv()
    with_edges(
        xb.at[0], own,
        erecv[0].astype(F32).reshape(rows, 8, width), erecv[1].astype(F32).reshape(rows, 8, width),
    )
    for copy in row_copies(1) + row_copies(2):
        copy.start()

    def row_mask(first, count):
        on = mp[pl.ds(first, count)][:, :1, :]
        return jnp.concatenate([on, on], axis=2)

    def norm(cells, blk):
        mean_of = jnp.full((width, width), 1.0 / width, BF)
        off = cells.astype(F32) - jnp.dot(cells, mean_of, preferred_element_type=F32)
        var = jnp.dot((off * off).astype(BF), mean_of, preferred_element_type=F32)
        return (off * lax.rsqrt(var + 1e-05) * gain[pl.ds(blk, 1)]).astype(BF)

    column = lax.broadcasted_iota(jnp.int32, (1, wide, 1), 1)
    inside = (column >= EDGE) & (column < EDGE + cols)

    def block(blk):
        x = xb.at[blk]
        w1_copy, w2_copy, wqkv_copy, wo_copy = weight_copies(blk)
        band = lat + blk * (band_1 - lat)
        sector = lon + blk * (sector_1 - lon)
        parity = sector % 2
        first_row = band % 2 * rows

        def arrived(place):
            source = row_at(place)

            @pl.when(elsewhere(source))
            def _():
                state_copy(att.at[0, 0], 1, place, h_send.at[0, 0], (lat, sibling)).wait_recv()

        def state_copy(src, to_blk, place, send, to):
            return remote(src, xb.at[to_blk, place], send, x_recv.at[to_blk, place], to)

        w1_copy.wait()

        @pl.when(blk == 1)
        def _():
            each(rows, lambda r: arrived(EDGE + r))

        def first(start):
            got = conv(x, start, EDGE, 1, w1.at[blk])
            got = jax.nn.gelu(got).reshape(EDGE, wide, width) * row_mask(first_row + start + 1, EDGE)
            hb[pl.ds(start, EDGE)] = got.astype(BF)

        each(2, lambda k: first(EDGE * (1 + k)))

        @pl.when(blk == 0)
        def _():
            for n in range(3):
                for copy in row_copies(n):
                    copy.wait_recv()
            mask_copy().wait_recv()

        @pl.when(blk == 1)
        def _():
            each(EDGE, arrived)
            each(EDGE, lambda r: arrived(EDGE + rows + r))

        @pl.when(band == 0)
        def _():
            x[0:EDGE] = jnp.zeros((EDGE, wide, width), BF)

        @pl.when(band == lats - 1)
        def _():
            x[EDGE + rows :] = jnp.zeros((EDGE, wide, width), BF)

        each(2, lambda k: first(3 * EDGE * k))

        w2_copy.wait()

        def row_copy(r):
            return remote(
                nself.at[blk, r], nbuf.at[blk, parity, sector // 2], f_send.at[blk, r],
                f_recv.at[blk, sector // 2], (band, r * CORES + parity),
            )

        def second(k):
            a = across(k) * 2
            got = jax.nn.gelu(conv(hb, a, 2, 2, w2.at[blk])).reshape(2, wide, width)
            got = (x[pl.ds(a + EDGE, 2)].astype(F32) + got) * row_mask(first_row + a + EDGE, 2)
            nself[blk, pl.ds(a, 2)] = got.astype(BF)
            for i in range(2):
                r = a + i
                far = elsewhere((band, r * CORES + parity))

                @pl.when(far)
                def _():
                    row_copy(r).start()

                @pl.when(jnp.logical_not(far))
                def _():
                    nbuf[blk, parity, sector // 2] = nself[blk, r]

        each(groups, second)

        def half_copy(i):
            slot = nbuf.at[blk, core, i]
            return remote(slot, slot, s_send.at[blk, i], s_recv.at[blk, i], (lat, sibling))

        def pass_on(k):
            i = across(k // 2) * 2 + k % 2

            @pl.when(elsewhere(placed(blk, lat, i * CORES + core)))
            def _():
                remote(
                    nself.at[blk, i], nbuf.at[blk, core, i], f_send.at[blk, i], f_recv.at[blk, i],
                    (lat, sibling),
                ).wait_recv()

            half_copy(i).start()

        each(chips, pass_on)

        wqkv_copy.wait()
        first_head = lax.broadcasted_iota(jnp.int32, (1, 1, 2 * head_dim), 2) < head_dim
        ones = jnp.where(inside, 1.0, 0.0)

        def keys_values(t):
            side = (core + t) % CORES

            @pl.when(t == 1)
            def _():
                each(chips, lambda i: half_copy(i).wait_recv())

            cells = norm(nbuf[blk, side].reshape(half, width), blk)
            cells = jnp.where(inside, cells.reshape(chips, wide, width), jnp.zeros((), BF))
            cells = cells.reshape(half, width)
            both = jnp.dot(cells, wqkv[blk, :, width:], preferred_element_type=F32)
            kb[side] = both[:, :width].astype(BF).reshape(chips, wide, width)
            values = both[:, width:].reshape(chips, wide, width)
            for h in range(HEADS):
                pair = values[:, :, h // 2 * 2 * head_dim :][:, :, : 2 * head_dim]
                keep = first_head if h % 2 == 0 else ~first_head
                vx[h, side] = jnp.where(keep, pair, ones).astype(BF)

        each(CORES, keys_values)

        qm[...] = nbuf[blk, core]

        def join(i):
            before, after = (i + chips - 1 + core) % chips, (i + core) % chips
            from_left = shifted(nbuf[blk, 1 - core, pl.ds(before, 1)], wide - 8, 6)
            from_right = shifted(nbuf[blk, 1 - core, pl.ds(after, 1)], 0, 2)
            with_edges(qm, pl.ds(i, 1), from_left, from_right)

        each(chips, join)
        wo_copy.wait()

        def home_copy(i):
            to = placed(1 - blk, lat, i * CORES + core)
            return to, state_copy(att.at[blk, i], blk + 1, EDGE + chip, h_send.at[blk, i], to)

        beside_at = chip - (rows - EDGE) + (7 - chip) // 5 * 16

        def halo_copy(i):
            to = place_1(beside, i * CORES + core)
            return to, state_copy(att.at[0, i], 1, beside_at, n_send.at[i], to)

        def attend(k):
            a = across(k) * 2
            cells = qm[pl.ds(a, 2)].reshape(2 * wide, width)
            scale = math.log2(math.e) / math.sqrt(head_dim)
            query = jnp.dot(norm(cells, blk), wqkv[blk, :, :width], preferred_element_type=F32)
            query = (query * scale).astype(BF)
            low_lane = lax.broadcasted_iota(jnp.int32, (1, 2 * head_dim), 1) < head_dim
            zero = jnp.zeros((), BF)
            attended = []
            for p in range(HEADS // 2):
                span = slice(p * 2 * head_dim, (p + 1) * 2 * head_dim)
                both = query[:, span]
                lhs = jnp.concatenate(
                    [jnp.where(low_lane, both, zero), jnp.where(low_lane, zero, both)], axis=0
                )
                keys = kb[:, :, :, span].reshape(CORES * half, 2 * head_dim)
                scores = lax.dot_general(
                    lhs, keys, (((1,), (1,)), ((), ())), preferred_element_type=F32
                )
                expo = jnp.exp2(scores).astype(BF)
                got = []
                for e in range(2):
                    values = vx[2 * p + e].reshape(CORES * half, 2 * head_dim)
                    part = jnp.dot(
                        expo[e * 2 * wide : (e + 1) * 2 * wide], values, preferred_element_type=F32
                    )
                    got.append(part / pltpu.roll(part, head_dim, 1))
                attended.append(jnp.where(low_lane, got[0], got[1]).astype(BF))
            update = jnp.dot(
                jnp.concatenate(attended, axis=1), wo[blk], preferred_element_type=F32
            )
            state = (cells.astype(F32) + update).reshape(2, wide, width) * row_mask(EDGE + y_hi * rows + chip, 1)
            att[blk, pl.ds(a, 2)] = state.astype(BF)
            for n in range(2):
                i = a + n
                to, copy = home_copy(i)
                far = elsewhere(to)

                @pl.when(far)
                def _():
                    copy.start()

                @pl.when(jnp.logical_not(far))
                def _():
                    xb[blk + 1, EDGE + chip] = att[blk, i]

                @pl.when((blk == 0) & is_halo)
                def _():
                    to, copy = halo_copy(i)
                    far = elsewhere(to)

                    @pl.when(far)
                    def _():
                        copy.start()

                    @pl.when(jnp.logical_not(far))
                    def _():
                        xb[1, beside_at] = att[0, i]

        each(groups, attend)

        def left_here(i):
            @pl.when(elsewhere((band, i * CORES + parity)))
            def _():
                row_copy(i).wait_send()

            half_copy(i).wait_send()
            to, copy = home_copy(i)

            @pl.when(elsewhere(to))
            def _():
                copy.wait_send()

            @pl.when((blk == 0) & is_halo)
            def _():
                to, copy = halo_copy(i)

                @pl.when(elsewhere(to))
                def _():
                    copy.wait_send()

        each(chips, left_here)

    each(BLOCKS, block)

    for copy in edge_copies() + row_copies(0) + row_copies(1) + row_copies(2) + [mask_copy()]:
        copy.wait_send()

    def come_home(r):
        @pl.when(r != chip)
        def _():
            remote(
                att.at[0, 0], xb.at[BLOCKS, EDGE + r], h_send.at[0, 0], x_recv.at[BLOCKS, EDGE + r],
                (lat, sibling),
            ).wait_recv()

    each(rows, come_home)
    out[...] = xb[BLOCKS, own]


def body(fields, lat_mask, conv_first, conv_second, norm_gain, qkv_weight, out_weight):
    rows, cols, width = fields.shape
    wide = cols + 2 * EDGE
    chips = lax.axis_size("lon") // CORES
    head_dim = width // HEADS
    vmem = pl.BlockSpec(memory_space=pltpu.VMEM)
    hbm = pl.BlockSpec(memory_space=pl.ANY)
    dma = pltpu.SemaphoreType.DMA
    wide_out = pl.pallas_call(
        kernel,
        out_shape=jax.ShapeDtypeStruct((rows, wide, width), BF),
        in_specs=[vmem, pl.BlockSpec(memory_space=pltpu.SMEM), hbm, hbm, vmem, hbm, hbm],
        out_specs=vmem,
        scratch_shapes=[
            pltpu.VMEM(conv_first.shape, BF),
            pltpu.VMEM(conv_second.shape, BF),
            pltpu.VMEM(qkv_weight.shape, BF),
            pltpu.VMEM(out_weight.shape, BF),
            pltpu.VMEM((rows, wide, width), F32),
            pltpu.VMEM((BLOCKS + 1, rows + 2 * EDGE, wide, width), BF),
            pltpu.VMEM((rows + 4, wide, width), BF),
            pltpu.VMEM((2 * rows + 2 * EDGE, 8, width // 2), F32),
            pltpu.VMEM((2, rows * 8, width), BF),
            pltpu.VMEM((2, rows * 8, width), BF),
            pltpu.VMEM((BLOCKS, rows, wide, width), BF),
            pltpu.VMEM((BLOCKS, CORES, chips, wide, width), BF),
            pltpu.VMEM((chips, wide, width), BF),
            pltpu.VMEM((CORES, chips, wide, width), BF),
            pltpu.VMEM((HEADS, CORES, chips, wide, 2 * head_dim), BF),
            pltpu.VMEM((BLOCKS, chips, wide, width), BF),
            dma((4, BLOCKS)),
            dma((2,)),
            dma((2,)),
            dma((3, 2)),
            dma((3, 2)),
            dma((2,)),
            dma((BLOCKS, rows)),
            dma((BLOCKS, chips)),
            dma((BLOCKS, chips)),
            dma((BLOCKS, chips)),
            dma((BLOCKS, chips)),
            dma((chips,)),
            dma((BLOCKS + 1, rows + 2 * EDGE)),
        ],
        compiler_params=pltpu.CompilerParams(
            collective_id=0, has_side_effects=True, vmem_limit_bytes=60 * 1024 * 1024
        ),
    )(fields, lat_mask, conv_first, conv_second, norm_gain, qkv_weight, out_weight)
    return wide_out[:, EDGE : EDGE + cols]


def solution(mesh):
    placed = (P("lat", "lon", None), P("lat"), P(), P(), P(), P(), P())
    return jax.shard_map(
        body, mesh=mesh, in_specs=placed, out_specs=P("lat", "lon", None), check_vma=False
    )
```

time: 83.1 us -> 76.2 us (0.917)
  Pallas kernels: 77.4 us -> 72.2 us
  local copies, waits for them, and re-layouts: 5.51 us -> 3.83 us
    pallas_call x1, Pallas kernels: 77.4 us -> 72.2 us  [body(): pl.pallas_call(kernel, out_shape=jax.ShapeDtypeStruct((rows, wide, width)...]
    unnamed x7 -> x1, local copies, waits for them, and re-layouts: 3.79 us -> 1.79 us
    slice x2, local copies, waits for them, and re-layouts: 1.04 us -> 2.03 us  [body(): return wide_out[:, EDGE:EDGE + cols]]
where the time goes in v2:
time: 76.2 us; the launch traced here: 76.1 us
  Pallas kernels  72.2 us (95%)
  local copies, waits for them, and re-layouts  3.83 us (5%)
    pallas_call x1, Pallas kernels, body(): pl.pallas_call(kernel, out_shape=jax.ShapeDtypeStruct((rows, wide, width)...  72.2 us
    slice x2, local copies, waits for them, and re-layouts, body(): return wide_out[:, EDGE:EDGE + cols]  2.03 us
    unnamed x1, local copies, waits for them, and re-layouts  1.79 us

profile of v2, /device:TPU:1, one launch (start us, length us, event | category | flops | bytes accessed | tf_op | source)
XLA Modules:
  0.0 76.1 jit_solution(16759732277848178348)
XLA Ops:
  0.0 1.8 %copy.8.fields = bf16[8,90,256]{2,1,0:T(8,128)(2,1)} copy(bf16[8,90,256]{2,0,1:T(8,128)(2,1)} %param.7) | data formatting | bytes 737280 | tf_op args[0]
  1.8 72.2 %shard_map.73 = bf16[8,96,256]{2,1,0:T(8,128)(2,1)} custom-call(bf16[8,90,256]{2,1,0:T(8,128)(2,1)} %copy.8.fields, s32[8]{0:T(128)} %mask.1, bf16[2,3,3,256,256]{4,3,2,1,0:T(8,128)(2,1)} %w1_hbm.1, bf16[2,3,3,256,256]{4,3,2,1,0:T(8,128)(2,1)} %w2_hbm.1, f32[2,256]{1,0:T(2,128)} %gain.1, bf16[2,256,768]{2,1,0:T(8,128)(2,1)} %wqkv_hbm.1, ...), custom_call_target="tpu_custom_call" | custom-call | tf_op jit(solution)/shard_map/pallas_call | solution.py:446
  74.0 1.1 %slice.3 = bf16[8,90,256]{2,1,0:T(8,128)(2,1)S(1)} slice(bf16[8,96,256]{2,1,0:T(8,128)(2,1)} %shard_map.73), slice={[0:8], [3:93], [0:256]} | slice | bytes 737280 | tf_op jit(solution)/shard_map/slice | solution.py:486
  75.1 0.9 %copy.9 = bf16[8,90,256]{2,0,1:T(8,128)(2,1)} copy(bf16[8,90,256]{2,1,0:T(8,128)(2,1)S(1)} %slice.3) | data formatting | bytes 737280 | tf_op jit(solution)/shard_map/slice | solution.py:486

commit v3 on v2

--- a/solution.py
+++ b/solution.py
@@ -51,10 +51,10 @@
 
 def kernel(
     fields, mask, w1_hbm, w2_hbm, gain, wqkv_hbm, wo_hbm, out,
-    w1, w2, wqkv, wo, xs, xb, hb, mp, epack, erecv, nself, nbuf, qm, kb, vx, att,
-    wsem, e_send, e_recv, l_send, l_recv, m_sem, f_send, f_recv, s_send, s_recv, h_send, n_send, x_recv,
+    w1, w2, wqkv, wo, xs, xb, hb, mp, epack, erecv, nself, nbuf, qm, qb, kb, vx, att,
+    wsem, e_send, e_recv, l_send, l_recv, m_sem, f_send, f_recv, s_send, s_recv, h_send, x_recv,
 ):
-    rows, cols, width = fields.shape
+    cols, rows, width = fields.shape
     wide = cols + 2 * EDGE
     head_dim = width // HEADS
     lats, lons = lax.axis_size("lat"), lax.axis_size("lon")
@@ -103,18 +103,14 @@
     def count(to):
         return jnp.where(elsewhere(to), 1, 0)
 
-    def row_at(place):
-        row = place - EDGE + rows
-        return (band_1 + row // rows - 1 + lats) % lats, row % rows * CORES + sector_1 % 2
-
-    beside = (lat + lats + chip // 5 - (7 - chip) // 5) % lats
-    is_halo = (chip < EDGE) | (chip >= rows - EDGE)
-
-    for to in ((up, lon), (down, lon), (lat, left), (lat, right), (lat, sibling)):
+    up_1 = place_1((band_1 + lats - 1) % lats, sector_1)
+    down_1 = place_1((band_1 + 1) % lats, sector_1)
+
+    for to in ((up, lon), (down, lon), (lat, left), (lat, right), (lat, sibling), up_1, down_1):
         greet(to)
     each(chips, lambda i: greet((lat, i * CORES + core)))
     each(chips, lambda i: greet(place_1(lat, i * CORES + core)))
-    each(rows + 2 * EDGE, lambda place: greet(row_at(place)))
+    each(rows, lambda r: greet((band_1, r * CORES + sector_1 % 2)))
 
     def weight_copies(blk):
         return [
@@ -128,23 +124,23 @@
         for copy in weight_copies(blk):
             copy.start()
 
-    xs[...] = jnp.zeros_like(xs)
+    xs[0:EDGE] = jnp.zeros((EDGE, rows, width), F32)
+    xs[EDGE + cols :] = jnp.zeros((EDGE, rows, width), F32)
+    xs[EDGE : EDGE + cols] = fields[...].astype(F32)
+    own = pl.ds(EDGE, rows)
     for a in range(rows):
         on = mask[a].astype(F32)
         mp[EDGE + y_hi * rows + a] = jnp.full(mp.shape[1:], on, F32)
-        xs[a, EDGE : EDGE + cols, :] = fields[a].astype(F32) * on
-    own = pl.ds(EDGE, rows)
-    xb[0, own] = xs[...].astype(BF)
+        xb[0, EDGE + a] = (xs[:, a, :] * on).astype(BF)
     mp[0:EDGE] = jnp.full((EDGE,) + mp.shape[1:], jnp.where(z > 0, 1.0, 0.0), F32)
     mp[EDGE + 2 * rows :] = jnp.full((EDGE,) + mp.shape[1:], jnp.where(z < lats // 2 - 1, 1.0, 0.0), F32)
     epack[0] = shifted(xb[0, own], 0, 2).reshape(rows * 8, width).astype(BF)
     epack[1] = shifted(xb[0, own], wide - 8, 6).reshape(rows * 8, width).astype(BF)
 
-    heard = 5
+    heard = 7
     for i in range(chips):
         heard += count((lat, i * CORES + core)) + count(place_1(lat, i * CORES + core))
         heard += count((band_1, i * CORES + sector_1 % 2))
-        heard += jnp.where(is_halo, count(place_1(beside, i * CORES + core)), 0)
     pl.semaphore_wait(barrier, heard)
 
     def mask_copy():
@@ -158,12 +154,13 @@
         ]
 
     def row_copies(n):
-        columns = (pl.ds(16, wide - 32), pl.ds(0, 16), pl.ds(wide - 16, 16))[n]
-        top, bottom = xb.at[0, pl.ds(EDGE, EDGE), columns], xb.at[0, pl.ds(rows, EDGE), columns]
-        above, below = xb.at[0, pl.ds(0, EDGE), columns], xb.at[0, pl.ds(EDGE + rows, EDGE), columns]
+        blk, to_up, to_down = (1, up_1, down_1) if n == 3 else (0, (up, lon), (down, lon))
+        columns = (pl.ds(16, wide - 32), pl.ds(0, 16), pl.ds(wide - 16, 16), pl.ds(0, wide))[n]
+        top, bottom = xb.at[blk, pl.ds(EDGE, EDGE), columns], xb.at[blk, pl.ds(rows, EDGE), columns]
+        above, below = xb.at[blk, pl.ds(0, EDGE), columns], xb.at[blk, pl.ds(EDGE + rows, EDGE), columns]
         return [
-            remote(top, below, l_send.at[n, 0], l_recv.at[n, 1], (up, lon)),
-            remote(bottom, above, l_send.at[n, 1], l_recv.at[n, 0], (down, lon)),
+            remote(top, below, l_send.at[n, 0], l_recv.at[n, 1], to_up),
+            remote(bottom, above, l_send.at[n, 1], l_recv.at[n, 0], to_down),
         ]
 
     for copy in edge_copies() + row_copies(0):
@@ -192,6 +189,11 @@
     column = lax.broadcasted_iota(jnp.int32, (1, wide, 1), 1)
     inside = (column >= EDGE) & (column < EDGE + cols)
 
+    def state_copy(blk, i, to_blk, r, to):
+        return remote(
+            att.at[blk, i], xb.at[to_blk, EDGE + r], h_send.at[blk, i], x_recv.at[to_blk, r], to
+        )
+
     def block(blk):
         x = xb.at[blk]
         w1_copy, w2_copy, wqkv_copy, wo_copy = weight_copies(blk)
@@ -200,21 +202,21 @@
         parity = sector % 2
         first_row = band % 2 * rows
 
-        def arrived(place):
-            source = row_at(place)
-
-            @pl.when(elsewhere(source))
+        def arrived(r):
+            @pl.when(elsewhere((band_1, r * CORES + sector_1 % 2)))
             def _():
-                state_copy(att.at[0, 0], 1, place, h_send.at[0, 0], (lat, sibling)).wait_recv()
-
-        def state_copy(src, to_blk, place, send, to):
-            return remote(src, xb.at[to_blk, place], send, x_recv.at[to_blk, place], to)
+                state_copy(0, 0, 1, r, (lat, sibling)).wait_recv()
 
         w1_copy.wait()
 
         @pl.when(blk == 1)
         def _():
-            each(rows, lambda r: arrived(EDGE + r))
+            to_up, to_down = row_copies(3)
+            each(EDGE, arrived)
+            to_up.start()
+            each(EDGE, lambda r: arrived(rows - EDGE + r))
+            to_down.start()
+            each(rows - 2 * EDGE, lambda r: arrived(EDGE + r))
 
         def first(start):
             got = conv(x, start, EDGE, 1, w1.at[blk])
@@ -232,8 +234,8 @@
 
         @pl.when(blk == 1)
         def _():
-            each(EDGE, arrived)
-            each(EDGE, lambda r: arrived(EDGE + rows + r))
+            for copy in row_copies(3):
+                copy.wait_recv()
 
         @pl.when(band == 0)
         def _():
@@ -325,22 +327,18 @@
         each(chips, join)
         wo_copy.wait()
 
+        norm_all = norm(qm[...].reshape(half, width), blk)
+        query = jnp.dot(norm_all, wqkv[blk, :, :width], preferred_element_type=F32)
+        scale = math.log2(math.e) / math.sqrt(head_dim)
+        qb[...] = (query * scale).astype(BF).reshape(chips, wide, width)
+
         def home_copy(i):
             to = placed(1 - blk, lat, i * CORES + core)
-            return to, state_copy(att.at[blk, i], blk + 1, EDGE + chip, h_send.at[blk, i], to)
-
-        beside_at = chip - (rows - EDGE) + (7 - chip) // 5 * 16
-
-        def halo_copy(i):
-            to = place_1(beside, i * CORES + core)
-            return to, state_copy(att.at[0, i], 1, beside_at, n_send.at[i], to)
+            return to, state_copy(blk, i, blk + 1, chip, to)
 
         def attend(k):
             a = across(k) * 2
-            cells = qm[pl.ds(a, 2)].reshape(2 * wide, width)
-            scale = math.log2(math.e) / math.sqrt(head_dim)
-            query = jnp.dot(norm(cells, blk), wqkv[blk, :, :width], preferred_element_type=F32)
-            query = (query * scale).astype(BF)
+            query = qb[pl.ds(a, 2)].reshape(2 * wide, width)
             low_lane = lax.broadcasted_iota(jnp.int32, (1, 2 * head_dim), 1) < head_dim
             zero = jnp.zeros((), BF)
             attended = []
@@ -366,7 +364,8 @@
             update = jnp.dot(
                 jnp.concatenate(attended, axis=1), wo[blk], preferred_element_type=F32
             )
-            state = (cells.astype(F32) + update).reshape(2, wide, width) * row_mask(EDGE + y_hi * rows + chip, 1)
+            state = qm[pl.ds(a, 2)].astype(F32) + update.reshape(2, wide, width)
+            state = state * row_mask(EDGE + y_hi * rows + chip, 1)
             att[blk, pl.ds(a, 2)] = state.astype(BF)
             for n in range(2):
                 i = a + n
@@ -381,58 +380,44 @@
                 def _():
                     xb[blk + 1, EDGE + chip] = att[blk, i]
 
-                @pl.when((blk == 0) & is_halo)
-                def _():
-                    to, copy = halo_copy(i)
-                    far = elsewhere(to)
-
-                    @pl.when(far)
-                    def _():
-                        copy.start()
-
-                    @pl.when(jnp.logical_not(far))
-                    def _():
-                        xb[1, beside_at] = att[0, i]
-
         each(groups, attend)
 
-        def left_here(i):
+    each(BLOCKS, block)
+
+    def sent(blk):
+        band = lat + blk * (band_1 - lat)
+        parity = (lon + blk * (sector_1 - lon)) % 2
+
+        def one(i):
             @pl.when(elsewhere((band, i * CORES + parity)))
             def _():
-                row_copy(i).wait_send()
-
-            half_copy(i).wait_send()
-            to, copy = home_copy(i)
-
-            @pl.when(elsewhere(to))
+                remote(
+                    nself.at[blk, i], nbuf.at[blk, core, i], f_send.at[blk, i], f_recv.at[blk, i], (lat, sibling)
+                ).wait_send()
+
+            slot = nbuf.at[blk, core, i]
+            remote(slot, slot, s_send.at[blk, i], s_recv.at[blk, i], (lat, sibling)).wait_send()
+
+            @pl.when(elsewhere(placed(1 - blk, lat, i * CORES + core)))
             def _():
-                copy.wait_send()
-
-            @pl.when((blk == 0) & is_halo)
-            def _():
-                to, copy = halo_copy(i)
-
-                @pl.when(elsewhere(to))
-                def _():
-                    copy.wait_send()
-
-        each(chips, left_here)
-
-    each(BLOCKS, block)
-
-    for copy in edge_copies() + row_copies(0) + row_copies(1) + row_copies(2) + [mask_copy()]:
+                state_copy(blk, i, blk + 1, chip, (lat, sibling)).wait_send()
+
+        each(chips, one)
+
+    each(BLOCKS, sent)
+
+    for copy in edge_copies() + sum((row_copies(n) for n in range(4)), []) + [mask_copy()]:
         copy.wait_send()
 
     def come_home(r):
         @pl.when(r != chip)
         def _():
-            remote(
-                att.at[0, 0], xb.at[BLOCKS, EDGE + r], h_send.at[0, 0], x_recv.at[BLOCKS, EDGE + r],
-                (lat, sibling),
-            ).wait_recv()
+            state_copy(0, 0, BLOCKS, r, (lat, sibling)).wait_recv()
 
     each(rows, come_home)
-    out[...] = xb[BLOCKS, own]
+    for a in range(rows):
+        xs[:, a, :] = xb[BLOCKS, EDGE + a].astype(F32)
+    out[...] = xs[EDGE : EDGE + cols].astype(BF)
 
 
 def body(fields, lat_mask, conv_first, conv_second, norm_gain, qkv_weight, out_weight):
@@ -443,9 +428,9 @@
     vmem = pl.BlockSpec(memory_space=pltpu.VMEM)
     hbm = pl.BlockSpec(memory_space=pl.ANY)
     dma = pltpu.SemaphoreType.DMA
-    wide_out = pl.pallas_call(
+    out = pl.pallas_call(
         kernel,
-        out_shape=jax.ShapeDtypeStruct((rows, wide, width), BF),
+        out_shape=jax.ShapeDtypeStruct((cols, rows, width), BF),
         in_specs=[vmem, pl.BlockSpec(memory_space=pltpu.SMEM), hbm, hbm, vmem, hbm, hbm],
         out_specs=vmem,
         scratch_shapes=[
@@ -453,7 +438,7 @@
             pltpu.VMEM(conv_second.shape, BF),
             pltpu.VMEM(qkv_weight.shape, BF),
             pltpu.VMEM(out_weight.shape, BF),
-            pltpu.VMEM((rows, wide, width), F32),
+            pltpu.VMEM((wide, rows, width), F32),
             pltpu.VMEM((BLOCKS + 1, rows + 2 * EDGE, wide, width), BF),
             pltpu.VMEM((rows + 4, wide, width), BF),
             pltpu.VMEM((2 * rows + 2 * EDGE, 8, width // 2), F32),
@@ -462,28 +447,28 @@
             pltpu.VMEM((BLOCKS, rows, wide, width), BF),
             pltpu.VMEM((BLOCKS, CORES, chips, wide, width), BF),
             pltpu.VMEM((chips, wide, width), BF),
+            pltpu.VMEM((chips, wide, width), BF),
             pltpu.VMEM((CORES, chips, wide, width), BF),
             pltpu.VMEM((HEADS, CORES, chips, wide, 2 * head_dim), BF),
             pltpu.VMEM((BLOCKS, chips, wide, width), BF),
             dma((4, BLOCKS)),
             dma((2,)),
             dma((2,)),
-            dma((3, 2)),
-            dma((3, 2)),
+            dma((4, 2)),
+            dma((4, 2)),
             dma((2,)),
             dma((BLOCKS, rows)),
             dma((BLOCKS, chips)),
             dma((BLOCKS, chips)),
             dma((BLOCKS, chips)),
             dma((BLOCKS, chips)),
-            dma((chips,)),
-            dma((BLOCKS + 1, rows + 2 * EDGE)),
+            dma((BLOCKS + 1, rows)),
         ],
         compiler_params=pltpu.CompilerParams(
             collective_id=0, has_side_effects=True, vmem_limit_bytes=60 * 1024 * 1024
         ),
-    )(fields, lat_mask, conv_first, conv_second, norm_gain, qkv_weight, out_weight)
-    return wide_out[:, EDGE : EDGE + cols]
+    )(jnp.transpose(fields, (1, 0, 2)), lat_mask, conv_first, conv_second, norm_gain, qkv_weight, out_weight)
+    return jnp.transpose(out, (1, 0, 2))
 
 
 def solution(mesh):

time: 76.2 us -> 73.8 us (0.969)
  local copies, waits for them, and re-layouts: 3.83 us -> 1.75 us
    slice x2 -> x0, local copies, waits for them, and re-layouts: 2.03 us -> none  [body(): return wide_out[:, EDGE:EDGE + cols]]
where the time goes in v3:
time: 73.8 us; the launch traced here: 73.7 us
  Pallas kernels  71.9 us (97%)
  local copies, waits for them, and re-layouts  1.75 us (2%)
    pallas_call x1, Pallas kernels, body(): pl.pallas_call(kernel, out_shape=jax.ShapeDtypeStruct((cols, rows, width)...  71.9 us
    unnamed x1, local copies, waits for them, and re-layouts  1.75 us

profile of v3, /device:TPU:1, one launch (start us, length us, event | category | flops | bytes accessed | tf_op | source)
XLA Modules:
  0.0 73.7 jit_solution(8092428238900528737)
XLA Ops:
  0.0 71.9 %shard_map.73 = bf16[90,8,256]{2,1,0:T(8,128)(2,1)} custom-call(bf16[90,8,256]{2,1,0:T(8,128)(2,1)} %bitcast.3, s32[8]{0:T(128)} %mask.1, bf16[2,3,3,256,256]{4,3,2,1,0:T(8,128)(2,1)} %w1_hbm.1, bf16[2,3,3,256,256]{4,3,2,1,0:T(8,128)(2,1)} %w2_hbm.1, f32[2,256]{1,0:T(2,128)} %gain.1, bf16[2,256,768]{2,1,0:T(8,128)(2,1)} %wqkv_hbm.1, bf16[2,256,256]{2,1,0:T(8,128)(2,1)} %wo_hbm.1), custom_call_target="tpu_custom_call" | custom-call | tf_op jit(solution)/shard_map/pallas_call | solution.py:431
  71.9 1.7 %copy.9 = bf16[8,90,256]{2,0,1:T(8,128)(2,1)} copy(bf16[8,90,256]{2,0,1:T(8,128)(2,1)} %bitcast.2) | data formatting | bytes 737280

commit v4 on v3

--- a/solution.py
+++ b/solution.py
@@ -50,9 +50,9 @@
 
 
 def kernel(
-    fields, mask, w1_hbm, w2_hbm, gain, wqkv_hbm, wo_hbm, out,
-    w1, w2, wqkv, wo, xs, xb, hb, mp, epack, erecv, nself, nbuf, qm, qb, kb, vx, att,
-    wsem, e_send, e_recv, l_send, l_recv, m_sem, f_send, f_recv, s_send, s_recv, h_send, x_recv,
+    fields_hbm, mask_hbm, w1_hbm, w2_hbm, gain_hbm, wqkv_hbm, wo_hbm, out,
+    fields, mask, gain, w1, w2, wqkv, wo, xs, xb, hb, mp, epack, erecv, nself, nbuf, qm, qb, kb, vx, att,
+    isem, wsem, e_send, e_recv, l_send, l_recv, m_sem, f_send, f_recv, s_send, s_recv, h_send, x_recv,
 ):
     cols, rows, width = fields.shape
     wide = cols + 2 * EDGE
@@ -100,17 +100,14 @@
         def _():
             pl.semaphore_signal(barrier, inc=1, device_id=to, device_id_type=MESH)
 
-    def count(to):
-        return jnp.where(elsewhere(to), 1, 0)
-
     up_1 = place_1((band_1 + lats - 1) % lats, sector_1)
     down_1 = place_1((band_1 + 1) % lats, sector_1)
 
-    for to in ((up, lon), (down, lon), (lat, left), (lat, right), (lat, sibling), up_1, down_1):
-        greet(to)
-    each(chips, lambda i: greet((lat, i * CORES + core)))
-    each(chips, lambda i: greet(place_1(lat, i * CORES + core)))
-    each(rows, lambda r: greet((band_1, r * CORES + sector_1 % 2)))
+    inputs = [
+        pltpu.make_async_copy(mask_hbm, mask, isem.at[0]),
+        pltpu.make_async_copy(fields_hbm, fields, isem.at[1]),
+        pltpu.make_async_copy(gain_hbm, gain, isem.at[2]),
+    ]
 
     def weight_copies(blk):
         return [
@@ -120,10 +117,18 @@
             pltpu.make_async_copy(wo_hbm.at[blk], wo.at[blk], wsem.at[3, blk]),
         ]
 
+    for copy in inputs:
+        copy.start()
     for blk in range(BLOCKS):
         for copy in weight_copies(blk):
             copy.start()
 
+    for to in ((up, lon), (down, lon), (lat, left), (lat, right), (lat, sibling)):
+        greet(to)
+    each(chips, lambda i: greet((lat, i * CORES + core)))
+
+    for copy in inputs:
+        copy.wait()
     xs[0:EDGE] = jnp.zeros((EDGE, rows, width), F32)
     xs[EDGE + cols :] = jnp.zeros((EDGE, rows, width), F32)
     xs[EDGE : EDGE + cols] = fields[...].astype(F32)
@@ -137,11 +142,7 @@
     epack[0] = shifted(xb[0, own], 0, 2).reshape(rows * 8, width).astype(BF)
     epack[1] = shifted(xb[0, own], wide - 8, 6).reshape(rows * 8, width).astype(BF)
 
-    heard = 7
-    for i in range(chips):
-        heard += count((lat, i * CORES + core)) + count(place_1(lat, i * CORES + core))
-        heard += count((band_1, i * CORES + sector_1 % 2))
-    pl.semaphore_wait(barrier, heard)
+    pl.semaphore_wait(barrier, 5 + chips - 1)
 
     def mask_copy():
         both = mp.at[pl.ds(EDGE + y_hi * rows, rows)]
@@ -245,8 +246,6 @@
         def _():
             x[EDGE + rows :] = jnp.zeros((EDGE, wide, width), BF)
 
-        each(2, lambda k: first(3 * EDGE * k))
-
         w2_copy.wait()
 
         def row_copy(r):
@@ -257,6 +256,11 @@
 
         def second(k):
             a = across(k) * 2
+
+            @pl.when(k < 2)
+            def _():
+                first(3 * EDGE * ((across(0) // 2 + k) % 2))
+
             got = jax.nn.gelu(conv(hb, a, 2, 2, w2.at[blk])).reshape(2, wide, width)
             got = (x[pl.ds(a + EDGE, 2)].astype(F32) + got) * row_mask(first_row + a + EDGE, 2)
             nself[blk, pl.ds(a, 2)] = got.astype(BF)
@@ -296,6 +300,12 @@
         first_head = lax.broadcasted_iota(jnp.int32, (1, 1, 2 * head_dim), 2) < head_dim
         ones = jnp.where(inside, 1.0, 0.0)
 
+        scale = math.log2(math.e) / math.sqrt(head_dim)
+
+        def set_query(cells):
+            query = jnp.dot(cells, wqkv[blk, :, :width], preferred_element_type=F32)
+            qb[...] = (query * scale).astype(BF).reshape(chips, wide, width)
+
         def keys_values(t):
             side = (core + t) % CORES
 
@@ -304,6 +314,11 @@
                 each(chips, lambda i: half_copy(i).wait_recv())
 
             cells = norm(nbuf[blk, side].reshape(half, width), blk)
+
+            @pl.when((t == 0) & (blk == BLOCKS - 1))
+            def _():
+                set_query(cells)
+
             cells = jnp.where(inside, cells.reshape(chips, wide, width), jnp.zeros((), BF))
             cells = cells.reshape(half, width)
             both = jnp.dot(cells, wqkv[blk, :, width:], preferred_element_type=F32)
@@ -312,11 +327,10 @@
             for h in range(HEADS):
                 pair = values[:, :, h // 2 * 2 * head_dim :][:, :, : 2 * head_dim]
                 keep = first_head if h % 2 == 0 else ~first_head
-                vx[h, side] = jnp.where(keep, pair, ones).astype(BF)
-
+                vx[h, side] = jnp.where(keep, pair, ones).astype(BF).reshape(vx.shape[2:])
+
+        qm[...] = nbuf[blk, core]
         each(CORES, keys_values)
-
-        qm[...] = nbuf[blk, core]
 
         def join(i):
             before, after = (i + chips - 1 + core) % chips, (i + core) % chips
@@ -324,13 +338,12 @@
             from_right = shifted(nbuf[blk, 1 - core, pl.ds(after, 1)], 0, 2)
             with_edges(qm, pl.ds(i, 1), from_left, from_right)
 
-        each(chips, join)
+        @pl.when(blk < BLOCKS - 1)
+        def _():
+            each(chips, join)
+            set_query(norm(qm[...].reshape(half, width), blk))
+
         wo_copy.wait()
-
-        norm_all = norm(qm[...].reshape(half, width), blk)
-        query = jnp.dot(norm_all, wqkv[blk, :, :width], preferred_element_type=F32)
-        scale = math.log2(math.e) / math.sqrt(head_dim)
-        qb[...] = (query * scale).astype(BF).reshape(chips, wide, width)
 
         def home_copy(i):
             to = placed(1 - blk, lat, i * CORES + core)
@@ -415,9 +428,7 @@
             state_copy(0, 0, BLOCKS, r, (lat, sibling)).wait_recv()
 
     each(rows, come_home)
-    for a in range(rows):
-        xs[:, a, :] = xb[BLOCKS, EDGE + a].astype(F32)
-    out[...] = xs[EDGE : EDGE + cols].astype(BF)
+    out[...] = xb[BLOCKS, own]
 
 
 def body(fields, lat_mask, conv_first, conv_second, norm_gain, qkv_weight, out_weight):
@@ -426,14 +437,17 @@
     chips = lax.axis_size("lon") // CORES
     head_dim = width // HEADS
     vmem = pl.BlockSpec(memory_space=pltpu.VMEM)
-    hbm = pl.BlockSpec(memory_space=pl.ANY)
+    hbm = pl.BlockSpec(memory_space=pltpu.HBM)
     dma = pltpu.SemaphoreType.DMA
-    out = pl.pallas_call(
+    wide_out = pl.pallas_call(
         kernel,
-        out_shape=jax.ShapeDtypeStruct((cols, rows, width), BF),
-        in_specs=[vmem, pl.BlockSpec(memory_space=pltpu.SMEM), hbm, hbm, vmem, hbm, hbm],
+        out_shape=jax.ShapeDtypeStruct((rows, wide, width), BF),
+        in_specs=[hbm] * 7,
         out_specs=vmem,
         scratch_shapes=[
+            pltpu.VMEM((cols, rows, width), BF),
+            pltpu.SMEM(lat_mask.shape, jnp.int32),
+            pltpu.VMEM(norm_gain.shape, F32),
             pltpu.VMEM(conv_first.shape, BF),
             pltpu.VMEM(conv_second.shape, BF),
             pltpu.VMEM(qkv_weight.shape, BF),
@@ -451,6 +465,7 @@
             pltpu.VMEM((CORES, chips, wide, width), BF),
             pltpu.VMEM((HEADS, CORES, chips, wide, 2 * head_dim), BF),
             pltpu.VMEM((BLOCKS, chips, wide, width), BF),
+            dma((3,)),
             dma((4, BLOCKS)),
             dma((2,)),
             dma((2,)),
@@ -468,7 +483,7 @@
             collective_id=0, has_side_effects=True, vmem_limit_bytes=60 * 1024 * 1024
         ),
     )(jnp.transpose(fields, (1, 0, 2)), lat_mask, conv_first, conv_second, norm_gain, qkv_weight, out_weight)
-    return jnp.transpose(out, (1, 0, 2))
+    return wide_out[:, EDGE : EDGE + cols]
 
 
 def solution(mesh):

time: 73.8 us -> 71.6 us (0.970)
  Pallas kernels: 71.9 us -> 69.4 us
    pallas_call x1, Pallas kernels: 71.9 us -> 69.4 us  [body(): pl.pallas_call(kernel, out_shape=jax.ShapeDtypeStruct((rows, wide, width)...]
    slice x0 -> x2, local copies, waits for them, and re-layouts: none -> 2.03 us  [body(): return wide_out[:, EDGE:EDGE + cols]]
    unnamed x1 -> x0, local copies, waits for them, and re-layouts: 1.75 us -> none
where the time goes in v4:
time: 71.6 us; the launch traced here: 71.5 us
  Pallas kernels  69.4 us (97%)
  local copies, waits for them, and re-layouts  2.03 us (3%)
    pallas_call x1, Pallas kernels, body(): pl.pallas_call(kernel, out_shape=jax.ShapeDtypeStruct((rows, wide, width)...  69.4 us
    slice x2, local copies, waits for them, and re-layouts, body(): return wide_out[:, EDGE:EDGE + cols]  2.03 us

profile of v4, /device:TPU:1, one launch (start us, length us, event | category | flops | bytes accessed | tf_op | source)
XLA Modules:
  0.0 71.5 jit_solution(2693691772757234691)
XLA Ops:
  0.0 69.4 %shard_map.73 = bf16[8,96,256]{2,1,0:T(8,128)(2,1)} custom-call(bf16[90,8,256]{2,1,0:T(8,128)(2,1)} %bitcast.1, s32[8]{0:T(128)} %mask_hbm.1, bf16[2,3,3,256,256]{4,3,2,1,0:T(8,128)(2,1)} %w1_hbm.1, bf16[2,3,3,256,256]{4,3,2,1,0:T(8,128)(2,1)} %w2_hbm.1, f32[2,256]{1,0:T(2,128)} %gain_hbm.1, bf16[2,256,768]{2,1,0:T(8,128)(2,1)} %wqkv_hbm.1, ...), custom_call_target="tpu_custom_call" | custom-call | tf_op jit(solution)/shard_map/pallas_call | solution.py:442
  69.4 1.1 %slice.3 = bf16[8,90,256]{2,1,0:T(8,128)(2,1)S(1)} slice(bf16[8,96,256]{2,1,0:T(8,128)(2,1)} %shard_map.73), slice={[0:8], [3:93], [0:256]} | slice | bytes 737280 | tf_op jit(solution)/shard_map/slice | solution.py:486
  70.5 0.9 %copy.8 = bf16[8,90,256]{2,0,1:T(8,128)(2,1)} copy(bf16[8,90,256]{2,1,0:T(8,128)(2,1)S(1)} %slice.3) | data formatting | bytes 737280 | tf_op jit(solution)/shard_map/slice | solution.py:486

commit v5 on v4

--- a/solution.py
+++ b/solution.py
@@ -441,7 +441,7 @@
     dma = pltpu.SemaphoreType.DMA
     wide_out = pl.pallas_call(
         kernel,
-        out_shape=jax.ShapeDtypeStruct((rows, wide, width), BF),
+        out_shape=pltpu.VMEM((rows, wide, width), BF),
         in_specs=[hbm] * 7,
         out_specs=vmem,
         scratch_shapes=[

time: 71.6 us -> 69.8 us (0.975)
  local copies, waits for them, and re-layouts: 2.03 us -> 1.04 us
    slice x2, local copies, waits for them, and re-layouts: 2.03 us -> 1.04 us  [body(): return wide_out[:, EDGE:EDGE + cols]]
    pallas_call x1, Pallas kernels: 69.4 us -> 68.7 us  [body(): pl.pallas_call(kernel, out_shape=pltpu.VMEM((rows, wide, width), BF), in_...]
where the time goes in v5:
time: 69.8 us; the launch traced here: 69.7 us
  Pallas kernels  68.7 us (98%)
  local copies, waits for them, and re-layouts  1.04 us (1%)
    pallas_call x1, Pallas kernels, body(): pl.pallas_call(kernel, out_shape=pltpu.VMEM((rows, wide, width), BF), in_...  68.7 us

profile of v5, /device:TPU:1, one launch (start us, length us, event | category | flops | bytes accessed | tf_op | source)
XLA Modules:
  0.0 69.7 jit_solution(18083333993148221641)
XLA Ops:
  0.0 68.7 %shard_map.73 = bf16[8,96,256]{2,1,0:T(8,128)(2,1)S(1)} custom-call(bf16[90,8,256]{2,1,0:T(8,128)(2,1)} %bitcast.1, s32[8]{0:T(128)} %mask_hbm.1, bf16[2,3,3,256,256]{4,3,2,1,0:T(8,128)(2,1)} %w1_hbm.1, bf16[2,3,3,256,256]{4,3,2,1,0:T(8,128)(2,1)} %w2_hbm.1, f32[2,256]{1,0:T(2,128)} %gain_hbm.1, bf16[2,256,768]{2,1,0:T(8,128)(2,1)} %wqkv_hbm.1, ...), custom_call_target="tpu_custom_call" | custom-call | tf_op jit(solution)/shard_map/pallas_call | solution.py:442
  68.7 0.1 slice.3
  68.8 0.9 %copy.8 = bf16[8,90,256]{2,0,1:T(8,128)(2,1)} copy(bf16[8,90,256]{2,1,0:T(8,128)(2,1)S(1)} %slice.3) | data formatting | bytes 737280 | tf_op jit(solution)/shard_map/slice | solution.py:486

commit v6 on v5

--- a/solution.py
+++ b/solution.py
@@ -226,25 +226,34 @@
 
         each(2, lambda k: first(EDGE * (1 + k)))
 
-        @pl.when(blk == 0)
-        def _():
-            for n in range(3):
-                for copy in row_copies(n):
-                    copy.wait_recv()
-            mask_copy().wait_recv()
-
-        @pl.when(blk == 1)
-        def _():
-            for copy in row_copies(3):
-                copy.wait_recv()
-
-        @pl.when(band == 0)
-        def _():
-            x[0:EDGE] = jnp.zeros((EDGE, wide, width), BF)
-
-        @pl.when(band == lats - 1)
-        def _():
-            x[EDGE + rows :] = jnp.zeros((EDGE, wide, width), BF)
+        def outer(side):
+            def ready(n):
+                @pl.when(side == 0)
+                def _():
+                    row_copies(n)[1].wait_recv()
+
+                @pl.when(side == 1)
+                def _():
+                    row_copies(n)[0].wait_recv()
+
+            @pl.when(blk == 0)
+            def _():
+                for n in range(3):
+                    ready(n)
+
+            @pl.when(blk == 1)
+            def _():
+                ready(3)
+
+            @pl.when((side == 0) & (band == 0))
+            def _():
+                x[0:EDGE] = jnp.zeros((EDGE, wide, width), BF)
+
+            @pl.when((side == 1) & (band == lats - 1))
+            def _():
+                x[EDGE + rows :] = jnp.zeros((EDGE, wide, width), BF)
+
+            first(3 * EDGE * side)
 
         w2_copy.wait()
 
@@ -254,12 +263,17 @@
                 f_recv.at[blk, sector // 2], (band, r * CORES + parity),
             )
 
+        @pl.when(blk == 0)
+        def _():
+            mask_copy().wait_recv()
+
         def second(k):
-            a = across(k) * 2
-
-            @pl.when(k < 2)
-            def _():
-                first(3 * EDGE * ((across(0) // 2 + k) % 2))
+            side = (1 - core + k // 2) % 2
+            a = side * 4 + (x_at + 1 + side + x_at // 2 + k) % 2 * 2
+
+            @pl.when(k % 2 == 0)
+            def _():
+                outer(side)
 
             got = jax.nn.gelu(conv(hb, a, 2, 2, w2.at[blk])).reshape(2, wide, width)
             got = (x[pl.ds(a + EDGE, 2)].astype(F32) + got) * row_mask(first_row + a + EDGE, 2)

time: 69.8 us -> 67.7 us (0.970)
  Pallas kernels: 68.7 us -> 66.5 us
    pallas_call x1, Pallas kernels: 68.7 us -> 66.5 us  [body(): pl.pallas_call(kernel, out_shape=pltpu.VMEM((rows, wide, width), BF), in_...]
where the time goes in v6:
time: 67.7 us; the launch traced here: 67.6 us
  Pallas kernels  66.5 us (98%)
  local copies, waits for them, and re-layouts  1.04 us (2%)
    pallas_call x1, Pallas kernels, body(): pl.pallas_call(kernel, out_shape=pltpu.VMEM((rows, wide, width), BF), in_...  66.5 us

profile of v6, /device:TPU:1, one launch (start us, length us, event | category | flops | bytes accessed | tf_op | source)
XLA Modules:
  0.0 67.6 jit_solution(16723787141288782234)
XLA Ops:
  0.0 66.5 %shard_map.73 = bf16[8,96,256]{2,1,0:T(8,128)(2,1)S(1)} custom-call(bf16[90,8,256]{2,1,0:T(8,128)(2,1)} %bitcast.1, s32[8]{0:T(128)} %mask_hbm.1, bf16[2,3,3,256,256]{4,3,2,1,0:T(8,128)(2,1)} %w1_hbm.1, bf16[2,3,3,256,256]{4,3,2,1,0:T(8,128)(2,1)} %w2_hbm.1, f32[2,256]{1,0:T(2,128)} %gain_hbm.1, bf16[2,256,768]{2,1,0:T(8,128)(2,1)} %wqkv_hbm.1, ...), custom_call_target="tpu_custom_call" | custom-call | tf_op jit(solution)/shard_map/pallas_call | solution.py:456
  66.5 0.1 slice.3
  66.6 0.9 %copy.8 = bf16[8,90,256]{2,0,1:T(8,128)(2,1)} copy(bf16[8,90,256]{2,1,0:T(8,128)(2,1)S(1)} %slice.3) | data formatting | bytes 737280 | tf_op jit(solution)/shard_map/slice | solution.py:500

commit v7 on v6

--- a/solution.py
+++ b/solution.py
@@ -103,6 +103,10 @@
     up_1 = place_1((band_1 + lats - 1) % lats, sector_1)
     down_1 = place_1((band_1 + 1) % lats, sector_1)
 
+    for to in ((up, lon), (down, lon), (lat, left), (lat, right), (lat, sibling)):
+        greet(to)
+    each(chips, lambda i: greet((lat, i * CORES + core)))
+
     inputs = [
         pltpu.make_async_copy(mask_hbm, mask, isem.at[0]),
         pltpu.make_async_copy(fields_hbm, fields, isem.at[1]),
@@ -122,10 +126,6 @@
     for blk in range(BLOCKS):
         for copy in weight_copies(blk):
             copy.start()
-
-    for to in ((up, lon), (down, lon), (lat, left), (lat, right), (lat, sibling)):
-        greet(to)
-    each(chips, lambda i: greet((lat, i * CORES + core)))
 
     for copy in inputs:
         copy.wait()
@@ -219,12 +219,12 @@
             to_down.start()
             each(rows - 2 * EDGE, lambda r: arrived(EDGE + r))
 
-        def first(start):
-            got = conv(x, start, EDGE, 1, w1.at[blk])
-            got = jax.nn.gelu(got).reshape(EDGE, wide, width) * row_mask(first_row + start + 1, EDGE)
-            hb[pl.ds(start, EDGE)] = got.astype(BF)
-
-        each(2, lambda k: first(EDGE * (1 + k)))
+        def first(start, count):
+            got = conv(x, start, count, 1, w1.at[blk])
+            got = jax.nn.gelu(got).reshape(count, wide, width) * row_mask(first_row + start + 1, count)
+            hb[pl.ds(start, count)] = got.astype(BF)
+
+        first(EDGE, rows - 2)
 
         def outer(side):
             def ready(n):
@@ -253,7 +253,7 @@
             def _():
                 x[EDGE + rows :] = jnp.zeros((EDGE, wide, width), BF)
 
-            first(3 * EDGE * side)
+            first(3 * EDGE * side, EDGE)
 
         w2_copy.wait()
 
@@ -316,9 +316,9 @@
 
         scale = math.log2(math.e) / math.sqrt(head_dim)
 
-        def set_query(cells):
-            query = jnp.dot(cells, wqkv[blk, :, :width], preferred_element_type=F32)
-            qb[...] = (query * scale).astype(BF).reshape(chips, wide, width)
+        def query(cells):
+            found = jnp.dot(cells, wqkv[blk, :, :width], preferred_element_type=F32)
+            return (found * scale).astype(BF).reshape(chips, -1, width)
 
         def keys_values(t):
             side = (core + t) % CORES
@@ -329,9 +329,9 @@
 
             cells = norm(nbuf[blk, side].reshape(half, width), blk)
 
-            @pl.when((t == 0) & (blk == BLOCKS - 1))
-            def _():
-                set_query(cells)
+            @pl.when(t == 0)
+            def _():
+                qb[...] = query(cells)
 
             cells = jnp.where(inside, cells.reshape(chips, wide, width), jnp.zeros((), BF))
             cells = cells.reshape(half, width)
@@ -354,8 +354,10 @@
 
         @pl.when(blk < BLOCKS - 1)
         def _():
-            each(chips, join)
-            set_query(norm(qm[...].reshape(half, width), blk))
+            for i in range(chips):
+                join(i)
+            for ends in (slice(0, 16), slice(wide - 16, wide)):
+                qb[:, ends] = query(norm(qm[:, ends].reshape(chips * 16, width), blk))
 
         wo_copy.wait()
 

time: 67.7 us -> 67.5 us (level)
  no operation moved by 1% of the time
where the time goes in v7:
time: 67.5 us
  Pallas kernels  66.4 us (98%)
  local copies, waits for them, and re-layouts  1.04 us (2%)
    pallas_call x1, Pallas kernels, body(): pl.pallas_call(kernel, out_shape=pltpu.VMEM((rows, wide, width), BF), in_...  66.4 us

profile of v7, /device:TPU:1, one launch (start us, length us, event | category | flops | bytes accessed | tf_op | source)
XLA Modules:
  0.0 67.5 jit_solution(18280538654922561299)
XLA Ops:
  0.0 66.4 %shard_map.73 = bf16[8,96,256]{2,1,0:T(8,128)(2,1)S(1)} custom-call(bf16[90,8,256]{2,1,0:T(8,128)(2,1)} %bitcast.1, s32[8]{0:T(128)} %mask_hbm.1, bf16[2,3,3,256,256]{4,3,2,1,0:T(8,128)(2,1)} %w1_hbm.1, bf16[2,3,3,256,256]{4,3,2,1,0:T(8,128)(2,1)} %w2_hbm.1, f32[2,256]{1,0:T(2,128)} %gain_hbm.1, bf16[2,256,768]{2,1,0:T(8,128)(2,1)} %wqkv_hbm.1, ...), custom_call_target="tpu_custom_call" | custom-call | tf_op jit(solution)/shard_map/pallas_call | solution.py:458
  66.4 0.1 slice.3
  66.5 0.9 %copy.8 = bf16[8,90,256]{2,0,1:T(8,128)(2,1)} copy(bf16[8,90,256]{2,1,0:T(8,128)(2,1)S(1)} %slice.3) | data formatting | bytes 737280 | tf_op jit(solution)/shard_map/slice | solution.py:502

commit v8 on v7

--- a/solution.py
+++ b/solution.py
@@ -190,6 +190,8 @@
     column = lax.broadcasted_iota(jnp.int32, (1, wide, 1), 1)
     inside = (column >= EDGE) & (column < EDGE + cols)
 
+    spare = BLOCKS + 1
+
     def state_copy(blk, i, to_blk, r, to):
         return remote(
             att.at[blk, i], xb.at[to_blk, EDGE + r], h_send.at[blk, i], x_recv.at[to_blk, r], to
@@ -363,7 +365,19 @@
 
         def home_copy(i):
             to = placed(1 - blk, lat, i * CORES + core)
-            return to, state_copy(blk, i, blk + 1, chip, to)
+            stays = jnp.where(elsewhere(to), 0, 1)
+            return remote(
+                att.at[blk, i],
+                xb.at[blk + 1 + stays * (spare - blk - 1), EDGE + chip + stays * (blk - EDGE - chip)],
+                h_send.at[blk, i],
+                x_recv.at[blk + 1 + stays * (spare - blk - 1), chip + stays * (blk - chip)],
+                (to[0], to[1] + stays * (sibling - to[1])),
+            )
+
+        def keep(i):
+            @pl.when(jnp.logical_not(elsewhere(placed(1 - blk, lat, i * CORES + core))))
+            def _():
+                xb[blk + 1, EDGE + chip] = att[blk, i]
 
         def attend(k):
             a = across(k) * 2
@@ -396,20 +410,16 @@
             state = qm[pl.ds(a, 2)].astype(F32) + update.reshape(2, wide, width)
             state = state * row_mask(EDGE + y_hi * rows + chip, 1)
             att[blk, pl.ds(a, 2)] = state.astype(BF)
-            for n in range(2):
-                i = a + n
-                to, copy = home_copy(i)
-                far = elsewhere(to)
-
-                @pl.when(far)
-                def _():
-                    copy.start()
-
-                @pl.when(jnp.logical_not(far))
-                def _():
-                    xb[blk + 1, EDGE + chip] = att[blk, i]
-
-        each(groups, attend)
+            home_copy(a).start()
+            home_copy(a + 1).start()
+
+        def attend_two(k):
+            attend(2 * k)
+            attend(2 * k + 1)
+
+        each(groups // 2, attend_two)
+        for n in range(2):
+            keep(x_at * 2 + n)
 
     each(BLOCKS, block)
 
@@ -427,9 +437,7 @@
             slot = nbuf.at[blk, core, i]
             remote(slot, slot, s_send.at[blk, i], s_recv.at[blk, i], (lat, sibling)).wait_send()
 
-            @pl.when(elsewhere(placed(1 - blk, lat, i * CORES + core)))
-            def _():
-                state_copy(blk, i, blk + 1, chip, (lat, sibling)).wait_send()
+            state_copy(blk, i, blk + 1, chip, (lat, sibling)).wait_send()
 
         each(chips, one)
 
@@ -444,6 +452,20 @@
             state_copy(0, 0, BLOCKS, r, (lat, sibling)).wait_recv()
 
     each(rows, come_home)
+
+    def spared(blk):
+        remote(
+            att.at[0, 0], xb.at[spare, blk], h_send.at[0, 0], x_recv.at[spare, blk], (lat, sibling)
+        ).wait_recv()
+
+    for n in range(2):
+        to = place_1(lat, (x_at * 2 + n) * CORES + 1 - core)
+
+        @pl.when((to[0] == lat) & (to[1] == sibling))
+        def _():
+            spared(0)
+
+    spared(1)
     out[...] = xb[BLOCKS, own]
 
 
@@ -469,7 +491,7 @@
             pltpu.VMEM(qkv_weight.shape, BF),
             pltpu.VMEM(out_weight.shape, BF),
             pltpu.VMEM((wide, rows, width), F32),
-            pltpu.VMEM((BLOCKS + 1, rows + 2 * EDGE, wide, width), BF),
+            pltpu.VMEM((BLOCKS + 2, rows + 2 * EDGE, wide, width), BF),
             pltpu.VMEM((rows + 4, wide, width), BF),
             pltpu.VMEM((2 * rows + 2 * EDGE, 8, width // 2), F32),
             pltpu.VMEM((2, rows * 8, width), BF),
@@ -493,7 +515,7 @@
             dma((BLOCKS, chips)),
             dma((BLOCKS, chips)),
             dma((BLOCKS, chips)),
-            dma((BLOCKS + 1, rows)),
+            dma((BLOCKS + 2, rows)),
         ],
         compiler_params=pltpu.CompilerParams(
             collective_id=0, has_side_effects=True, vmem_limit_bytes=60 * 1024 * 1024

time: 67.5 us -> 67.4 us (level)
  no operation moved by 1% of the time
where the time goes in v8:
time: 67.4 us; the launch traced here: 67.3 us
  Pallas kernels  66.2 us (98%)
  local copies, waits for them, and re-layouts  1.04 us (2%)
    pallas_call x1, Pallas kernels, body(): pl.pallas_call(kernel, out_shape=pltpu.VMEM((rows, wide, width), BF), in_...  66.2 us

profile of v8, /device:TPU:1, one launch (start us, length us, event | category | flops | bytes accessed | tf_op | source)
XLA Modules:
  0.0 67.3 jit_solution(6513614285088206114)
XLA Ops:
  0.0 66.2 %shard_map.73 = bf16[8,96,256]{2,1,0:T(8,128)(2,1)S(1)} custom-call(bf16[90,8,256]{2,1,0:T(8,128)(2,1)} %bitcast.1, s32[8]{0:T(128)} %mask_hbm.1, bf16[2,3,3,256,256]{4,3,2,1,0:T(8,128)(2,1)} %w1_hbm.1, bf16[2,3,3,256,256]{4,3,2,1,0:T(8,128)(2,1)} %w2_hbm.1, f32[2,256]{1,0:T(2,128)} %gain_hbm.1, bf16[2,256,768]{2,1,0:T(8,128)(2,1)} %wqkv_hbm.1, ...), custom_call_target="tpu_custom_call" | custom-call | tf_op jit(solution)/shard_map/pallas_call | solution.py:480
  66.2 0.1 slice.3
  66.3 0.9 %copy.8 = bf16[8,90,256]{2,0,1:T(8,128)(2,1)} copy(bf16[8,90,256]{2,1,0:T(8,128)(2,1)S(1)} %slice.3) | data formatting | bytes 737280 | tf_op jit(solution)/shard_map/slice | solution.py:524
